TPU v7x, 128 devices: a whole 4x4x4 slice. The times are simulated.
128 devices in a mesh: row: 8 (over z, core), col: 16 (over y, x).
Axes of the slice: x: 4, y: 4, z: 4, core: 2. Of those that a mesh axis runs over, the one named last changes fastest.
Arguments:
- vectors: bfloat16 [32768, 2048], P(('row', 'col')), may hold values from -6 to 6
- block_count: int32 [256], P(('row', 'col')), may hold values from 1 to 5, as said below
- block_cols: int32 [256, 5], P(('row', 'col')), may hold values from 0 to 255, as said below
- blocks: bfloat16 [256, 5, 128, 128], P(('row', 'col')), as said below
Outputs:
- hamiltonian_proj: float32 [2048, 2048], P('row', 'col')
- intersection_proj: float32 [2048, 2048], P('row', 'col')
Inputs may be any that keep to these rules, and one draw needn't show every extreme that they name: `block_count`: every block row stores its diagonal block; some block row stores all 5 slots. `block_cols`: slots 0 to block_count[i] - 1 of block row i hold distinct block columns, each at most 2 block rows from i in the periodic order modulo 256; the pattern is symmetric; the remaining slots hold i. `blocks`: the matrix H is symmetric; slots beyond block_count hold zeros.
All inputs are finite; a program needn't handle non-finite values.
Results may differ from a plain program's by a relative error of at most 0.0049.
Values may be sent and summed in bfloat16 or wider, within the bound.
A program may use at most 128 MiB of HBM per device.

v0:
```python
import math

import jax
import jax.numpy as jnp
from jax import lax
from jax.sharding import PartitionSpec as P

DEGREE = 8


filter_center = 0.25
filter_half = 1.75


def extended(x, sides, width):
    for axis, dim in sides:
        size, length = (lax.axis_size(axis), x.shape[dim])
        up = [(i, (i + 1) % size) for i in range(size)]
        down = [(j, i) for i, j in up]
        last = lax.slice_in_dim(x, length - width, length, axis=dim)
        initial = lax.slice_in_dim(x, 0, width, axis=dim)
        before = lax.ppermute(last, axis, up)
        after = lax.ppermute(initial, axis, down)
        x = jnp.concatenate([before, x, after], axis=dim)
    return x


def band_tiles(blocks, block_cols, block_count, first_block, total_blocks):
    local_blocks = blocks.shape[0]
    slot_count = blocks.shape[1]
    reach_blocks = (slot_count - 1) // 2
    relative = jnp.mod(block_cols - first_block + reach_blocks, total_blocks)
    row_ids = jnp.arange(local_blocks, dtype=jnp.int32)
    slot_ids = jnp.arange(slot_count, dtype=jnp.int32)
    in_use = slot_ids[None, :] < block_count[:, None]
    matches = jnp.logical_and(
        relative[:, :, None] == row_ids[:, None, None] + slot_ids[None, None, :], in_use[:, :, None]
    )
    selector = jnp.where(matches, 1.0, 0.0).astype(jnp.bfloat16)
    return jnp.einsum(
        "iko,ikab->ioab", selector, blocks, preferred_element_type=jnp.float32
    ).astype(jnp.bfloat16)


def apply_operator(source, tiles):
    local_blocks = tiles.shape[0]
    slot_count = tiles.shape[1]
    reach_blocks = (slot_count - 1) // 2
    height = tiles.shape[2]
    padded = extended(source, ((("row", "col"), 0),), reach_blocks * height)
    window = padded.reshape(local_blocks + 2 * reach_blocks, height, source.shape[1])
    summed = jnp.zeros((local_blocks, height, source.shape[1]), jnp.float32)
    for offset in range(slot_count):
        summed = summed + jnp.einsum(
            "iab,ibm->iam",
            tiles[:, offset],
            window[offset : offset + local_blocks],
            preferred_element_type=jnp.float32,
        )
    return summed.reshape(source.shape)


def body(vectors, block_count, block_cols, blocks):
    n_row = lax.axis_size("row")
    n_col = lax.axis_size("col")
    local_blocks = blocks.shape[0]
    total_blocks = local_blocks * n_row * n_col
    first_block = lax.axis_index(("row", "col")) * local_blocks
    tiles = band_tiles(blocks, block_cols, block_count, first_block, total_blocks)
    row_scale = 1.0 / math.sqrt(vectors.shape[0] * n_row * n_col)
    width = vectors.shape[1] // n_col
    previous = vectors
    current = (
        (apply_operator(previous, tiles) - filter_center * previous.astype(jnp.float32))
        / filter_half
    ).astype(jnp.bfloat16)
    for sweep_index in range(DEGREE - 1):
        product = apply_operator(current, tiles)
        following = (
            2.0 * (product - filter_center * current.astype(jnp.float32)) / filter_half
            - previous.astype(jnp.float32)
        ).astype(jnp.bfloat16)
        previous = current
        current = following
    applied = apply_operator(current, tiles).astype(jnp.bfloat16)
    vec_part, app_part = (
        lax.all_to_all(current, "col", split_axis=1, concat_axis=0, tiled=True),
        lax.all_to_all(applied, "col", split_axis=1, concat_axis=0, tiled=True),
    )
    paired = jnp.concatenate([app_part, vec_part], axis=1)
    partial_terms = lax.dot_general(
        lax.all_gather(vec_part, "col", axis=1, tiled=True),
        paired,
        (((0,), (0,)), ((), ())),
        preferred_element_type=jnp.float32,
    )
    summed = lax.psum_scatter(partial_terms, "row", scatter_dimension=0, tiled=True)
    hamiltonian_proj = summed[:, :width] * row_scale
    intersection_proj = summed[:, width:] * row_scale
    return (hamiltonian_proj, intersection_proj)


def solution(mesh):
    in_specs = (
        P(("row", "col"), None),
        P(("row", "col")),
        P(("row", "col"), None),
        P(("row", "col"), None, None, None),
    )
    out_specs = (P("row", "col"), P("row", "col"))
    return jax.shard_map(body, mesh=mesh, in_specs=in_specs, out_specs=out_specs, check_vma=False)
```

profile of v0, /device:TPU:16, one launch (start us, length us, event | category | flops | bytes accessed | tf_op | source)
XLA Modules:
  0.0 644.0 jit_solution(9392724763897527800)
XLA Ops:
  16.1 18.4 %collective-permute-done = bf16[256,2048]{1,0:T(8,128)(2,1)S(1)} collective-permute-done((bf16[256,2048]{1,0:T(8,128)(2,1)}, bf16[256,2048]{1,0:T(8,128)(2,1)S(1)}, u32[]{:S(2)}, u32[]{:S(2)}) %collective-permute-start) | collective-permute-done | bytes 1048608 | tf_op jit(solution)/shard_map/ppermute | solution.py:22
  51.4 17.7 %collective-permute-done.2 = bf16[256,2048]{0,1:T(8,128)(2,1)} collective-permute-done((bf16[256,2048]{0,1:T(8,128)(2,1)S(1)}, bf16[256,2048]{0,1:T(8,128)(2,1)}, u32[]{:S(2)}, u32[]{:S(2)}) %collective-permute-start.2) | collective-permute-done | bytes 1048608 | tf_op jit(solution)/shard_map/ppermute | solution.py:22
  87.7 3.7 convolution_add_fusion.21
  96.9 3.8 collective-permute-start.5
  105.1 16.6 %collective-permute-done.4 = bf16[256,2048]{0,1:T(8,128)(2,1)} collective-permute-done((bf16[256,2048]{0,1:T(8,128)(2,1)S(1)}, bf16[256,2048]{0,1:T(8,128)(2,1)}, u32[]{:S(2)}, u32[]{:S(2)}) %collective-permute-start.4) | collective-permute-done | bytes 1048608 | tf_op jit(solution)/shard_map/ppermute | solution.py:22
  140.4 3.7 convolution_add_fusion.18
  157.6 15.9 %collective-permute-done.6 = bf16[256,2048]{0,1:T(8,128)(2,1)} collective-permute-done((bf16[256,2048]{0,1:T(8,128)(2,1)S(1)}, bf16[256,2048]{0,1:T(8,128)(2,1)}, u32[]{:S(2)}, u32[]{:S(2)}) %collective-permute-start.6) | collective-permute-done | bytes 1048608 | tf_op jit(solution)/shard_map/ppermute | solution.py:22
  201.4 3.7 collective-permute-start.9
  209.5 14.8 %collective-permute-done.8 = bf16[256,2048]{0,1:T(8,128)(2,1)} collective-permute-done((bf16[256,2048]{0,1:T(8,128)(2,1)S(1)}, bf16[256,2048]{0,1:T(8,128)(2,1)}, u32[]{:S(2)}, u32[]{:S(2)}) %collective-permute-start.8) | collective-permute-done | bytes 1048608 | tf_op jit(solution)/shard_map/ppermute | solution.py:22
  245.5 3.7 convolution_add_fusion.12
  254.1 4.8 collective-permute-start.10
  263.3 16.2 %collective-permute-done.10 = bf16[256,2048]{0,1:T(8,128)(2,1)} collective-permute-done((bf16[256,2048]{0,1:T(8,128)(2,1)S(1)}, bf16[256,2048]{0,1:T(8,128)(2,1)}, u32[]{:S(2)}, u32[]{:S(2)}) %collective-permute-start.10) | collective-permute-done | bytes 1048608 | tf_op jit(solution)/shard_map/ppermute | solution.py:22
  300.4 3.7 convolution_add_fusion.9
  318.0 15.3 %collective-permute-done.12 = bf16[256,2048]{0,1:T(8,128)(2,1)} collective-permute-done((bf16[256,2048]{0,1:T(8,128)(2,1)S(1)}, bf16[256,2048]{0,1:T(8,128)(2,1)}, u32[]{:S(2)}, u32[]{:S(2)}) %collective-permute-start.12) | collective-permute-done | bytes 1048608 | tf_op jit(solution)/shard_map/ppermute | solution.py:22
  353.4 3.7 convolution_add_fusion.6
  362.0 5.5 collective-permute-start.14
  371.9 16.1 %collective-permute-done.14 = bf16[256,2048]{0,1:T(8,128)(2,1)} collective-permute-done((bf16[256,2048]{0,1:T(8,128)(2,1)S(1)}, bf16[256,2048]{0,1:T(8,128)(2,1)}, u32[]{:S(2)}, u32[]{:S(2)}) %collective-permute-start.14) | collective-permute-done | bytes 1048608 | tf_op jit(solution)/shard_map/ppermute | solution.py:22
  417.4 21.6 %all_to_all.35 = bf16[256,16,128]{0,2,1:T(8,128)(2,1)S(1)} all-to-all(bf16[256,16,128]{0,2,1:T(8,128)(2,1)S(1)} %bitcast.208), channel_id=1, replica_groups=mesh['row'=8,'col'=16] {'col'}, dimensions={1} | all-to-all | bytes 2097152 | tf_op jit(solution)/shard_map/all_to_all | solution.py:87
  441.1 3.7 collective-permute-start.17
  447.8 21.6 %collective-permute-done.16 = bf16[256,2048]{0,1:T(8,128)(2,1)} collective-permute-done((bf16[256,2048]{0,1:T(8,128)(2,1)S(1)}, bf16[256,2048]{0,1:T(8,128)(2,1)}, u32[]{:S(2)}, u32[]{:S(2)}) %collective-permute-start.16) | collective-permute-done | bytes 1048608 | tf_op jit(solution)/shard_map/ppermute | solution.py:22
  485.3 29.4 %all_to_all.36 = bf16[256,16,128]{2,0,1:T(8,128)(2,1)S(1)} all-to-all(bf16[256,16,128]{2,0,1:T(8,128)(2,1)S(1)} %copy.60), channel_id=1, replica_groups=mesh['row'=8,'col'=16] {'col'}, dimensions={1} | all-to-all | bytes 2097152 | tf_op jit(solution)/shard_map/all_to_all | solution.py:88
  514.6 73.5 %all-gather.2.cloned.1.call-done = bf16[4096,2048]{1,0:T(8,128)(2,1)} async-done(((bf16[4096,128]{1,0:T(8,128)(2,1)}), bf16[4096,2048]{1,0:T(8,128)(2,1)}) %all-gather.2.cloned.1.call-update) | async-done | bytes 16777232 | tf_op jit(solution)/shard_map/all_gather | solution.py:92
  588.1 9.7 %fusion.33 = f32[2048,256]{1,0:T(8,128)} fusion(bf16[4096,2048]{1,0:T(8,128)(2,1)} %all-gather.2.cloned.1.call-done, bf16[4096,128]{1,0:T(8,128)(2,1)S(1)} %bitcast.247, bf16[4096,128]{1,0:T(8,128)(2,1)S(1)} %bitcast.267), kind=kOutput, calls=%fused_computation.73 | convolution fusion | flops 4299161600 | bytes 20971520 | tf_op jit(solution)/shard_map/dot_general | solution.py:91
  597.9 37.4 %reduce-scatter.2.cloned.1.call-done = f32[256,256]{1,0:T(8,128)} async-done(((f32[2048,256]{1,0:T(8,128)}), f32[256,256]{1,0:T(8,128)}) %reduce-scatter.2.cloned.1.call-update) | async-done | bytes 262160 | tf_op jit(solution)/shard_map/reduce_scatter | solution.py:97
  (177 shorter events, 265.3 us)
Async XLA Ops:
  7.2 7.3 %copy-start = (bf16[2,5,128,128]{3,2,1,0:T(8,128)(2,1)S(1)}, bf16[2,5,128,128]{3,2,1,0:T(8,128)(2,1)}, u32[]{:S(2)}) copy-start(bf16[2,5,128,128]{3,2,1,0:T(8,128)(2,1)} %param.7) | copy-start | bytes 983044
  7.2 7.3 %copy-start.15 = (s32[2,5]{1,0:T(2,128)S(1)}, s32[2,5]{1,0:T(2,128)}, u32[]{:S(2)}) copy-start(s32[2,5]{1,0:T(2,128)} %param.6) | copy-start | bytes 124
  7.2 581.0 %all-gather.2.cloned.1.call-start = ((), (), s32[]{:S(2)}) async-start(), calls=%async_computation.3 | async-start | bytes 17825792 | tf_op jit(solution)/shard_map/all_gather | solution.py:92
  7.2 27.3 %collective-permute-start = (bf16[256,2048]{1,0:T(8,128)(2,1)}, bf16[256,2048]{1,0:T(8,128)(2,1)S(1)}, u32[]{:S(2)}, u32[]{:S(2)}) collective-permute-start(bf16[256,2048]{1,0:T(8,128)(2,1)} %param.4), channel_id=1, source_target_pairs={{0,1},{1,2},{2,3},{3,4},{4,5},{5,6},{6,7},{7,8},{8,9},{9,10},{10,1... | collective-permute-start | bytes 3145736 | tf_op jit(solution)/shard_map/ppermute | solution.py:22
  8.8 25.7 %collective-permute-start.1 = (bf16[256,2048]{1,0:T(8,128)(2,1)}, bf16[256,2048]{1,0:T(8,128)(2,1)S(1)}, u32[]{:S(2)}, u32[]{:S(2)}) collective-permute-start(bf16[256,2048]{1,0:T(8,128)(2,1)} %param.4), channel_id=1, source_target_pairs={{1,0},{2,1},{3,2},{4,3},{5,4},{6,5},{7,6},{8,7},{9,8},{10,9},{11,1... | collective-permute-start | bytes 3145736 | tf_op jit(solution)/shard_map/ppermute | solution.py:23
  42.8 26.3 %collective-permute-start.2 = (bf16[256,2048]{0,1:T(8,128)(2,1)S(1)}, bf16[256,2048]{0,1:T(8,128)(2,1)}, u32[]{:S(2)}, u32[]{:S(2)}) collective-permute-start(bf16[256,2048]{0,1:T(8,128)(2,1)S(1)} %fusion.13), channel_id=1, source_target_pairs={{0,1},{1,2},{2,3},{3,4},{4,5},{5,6},{6,7},{7,8},{8,9},{9,10},{10,1... | collective-permute-start | bytes 3145736 | tf_op jit(solution)/shard_map/ppermute | solution.py:22
  43.4 25.7 %collective-permute-start.3 = (bf16[256,2048]{0,1:T(8,128)(2,1)S(1)}, bf16[256,2048]{0,1:T(8,128)(2,1)S(1)}, u32[]{:S(2)}, u32[]{:S(2)}) collective-permute-start(bf16[256,2048]{0,1:T(8,128)(2,1)S(1)} %fusion.13), channel_id=1, source_target_pairs={{1,0},{2,1},{3,2},{4,3},{5,4},{6,5},{7,6},{8,7},{9,8},{10,9},{11,1... | collective-permute-start | bytes 3145736 | tf_op jit(solution)/shard_map/ppermute | solution.py:23
  96.3 25.4 %collective-permute-start.4 = (bf16[256,2048]{0,1:T(8,128)(2,1)S(1)}, bf16[256,2048]{0,1:T(8,128)(2,1)}, u32[]{:S(2)}, u32[]{:S(2)}) collective-permute-start(bf16[256,2048]{0,1:T(8,128)(2,1)S(1)} %fusion.14), channel_id=1, source_target_pairs={{0,1},{1,2},{2,3},{3,4},{4,5},{5,6},{6,7},{7,8},{8,9},{9,10},{10,1... | collective-permute-start | bytes 3145736 | tf_op jit(solution)/shard_map/ppermute | solution.py:22
  96.9 24.8 %collective-permute-start.5 = (bf16[256,2048]{0,1:T(8,128)(2,1)S(1)}, bf16[256,2048]{0,1:T(8,128)(2,1)S(1)}, u32[]{:S(2)}, u32[]{:S(2)}) collective-permute-start(bf16[256,2048]{0,1:T(8,128)(2,1)S(1)} %fusion.14), channel_id=1, source_target_pairs={{1,0},{2,1},{3,2},{4,3},{5,4},{6,5},{7,6},{8,7},{9,8},{10,9},{11,1... | collective-permute-start | bytes 3145736 | tf_op jit(solution)/shard_map/ppermute | solution.py:23
  149.0 24.5 %collective-permute-start.6 = (bf16[256,2048]{0,1:T(8,128)(2,1)S(1)}, bf16[256,2048]{0,1:T(8,128)(2,1)}, u32[]{:S(2)}, u32[]{:S(2)}) collective-permute-start(bf16[256,2048]{0,1:T(8,128)(2,1)S(1)} %fusion.17), channel_id=1, source_target_pairs={{0,1},{1,2},{2,3},{3,4},{4,5},{5,6},{6,7},{7,8},{8,9},{9,10},{10,1... | collective-permute-start | bytes 3145736 | tf_op jit(solution)/shard_map/ppermute | solution.py:22
  149.7 23.8 %collective-permute-start.7 = (bf16[256,2048]{0,1:T(8,128)(2,1)S(1)}, bf16[256,2048]{0,1:T(8,128)(2,1)S(1)}, u32[]{:S(2)}, u32[]{:S(2)}) collective-permute-start(bf16[256,2048]{0,1:T(8,128)(2,1)S(1)} %fusion.17), channel_id=1, source_target_pairs={{1,0},{2,1},{3,2},{4,3},{5,4},{6,5},{7,6},{8,7},{9,8},{10,9},{11,1... | collective-permute-start | bytes 3145736 | tf_op jit(solution)/shard_map/ppermute | solution.py:23
  200.7 23.5 %collective-permute-start.8 = (bf16[256,2048]{0,1:T(8,128)(2,1)S(1)}, bf16[256,2048]{0,1:T(8,128)(2,1)}, u32[]{:S(2)}, u32[]{:S(2)}) collective-permute-start(bf16[256,2048]{0,1:T(8,128)(2,1)S(1)} %fusion.20), channel_id=1, source_target_pairs={{0,1},{1,2},{2,3},{3,4},{4,5},{5,6},{6,7},{7,8},{8,9},{9,10},{10,1... | collective-permute-start | bytes 3145736 | tf_op jit(solution)/shard_map/ppermute | solution.py:22
  201.4 25.5 %collective-permute-start.9 = (bf16[256,2048]{0,1:T(8,128)(2,1)S(1)}, bf16[256,2048]{0,1:T(8,128)(2,1)S(1)}, u32[]{:S(2)}, u32[]{:S(2)}) collective-permute-start(bf16[256,2048]{0,1:T(8,128)(2,1)S(1)} %fusion.20), channel_id=1, source_target_pairs={{1,0},{2,1},{3,2},{4,3},{5,4},{6,5},{7,6},{8,7},{9,8},{10,9},{11,1... | collective-permute-start | bytes 3145736 | tf_op jit(solution)/shard_map/ppermute | solution.py:23
  254.1 25.4 %collective-permute-start.10 = (bf16[256,2048]{0,1:T(8,128)(2,1)S(1)}, bf16[256,2048]{0,1:T(8,128)(2,1)}, u32[]{:S(2)}, u32[]{:S(2)}) collective-permute-start(bf16[256,2048]{0,1:T(8,128)(2,1)S(1)} %fusion.23), channel_id=1, source_target_pairs={{0,1},{1,2},{2,3},{3,4},{4,5},{5,6},{6,7},{7,8},{8,9},{9,10},{10,1... | collective-permute-start | bytes 3145736 | tf_op jit(solution)/shard_map/ppermute | solution.py:22
  258.9 22.8 %collective-permute-start.11 = (bf16[256,2048]{0,1:T(8,128)(2,1)S(1)}, bf16[256,2048]{0,1:T(8,128)(2,1)S(1)}, u32[]{:S(2)}, u32[]{:S(2)}) collective-permute-start(bf16[256,2048]{0,1:T(8,128)(2,1)S(1)} %fusion.23), channel_id=1, source_target_pairs={{1,0},{2,1},{3,2},{4,3},{5,4},{6,5},{7,6},{8,7},{9,8},{10,9},{11,1... | collective-permute-start | bytes 3145736 | tf_op jit(solution)/shard_map/ppermute | solution.py:23
  309.0 24.3 %collective-permute-start.12 = (bf16[256,2048]{0,1:T(8,128)(2,1)S(1)}, bf16[256,2048]{0,1:T(8,128)(2,1)}, u32[]{:S(2)}, u32[]{:S(2)}) collective-permute-start(bf16[256,2048]{0,1:T(8,128)(2,1)S(1)} %fusion.26), channel_id=1, source_target_pairs={{0,1},{1,2},{2,3},{3,4},{4,5},{5,6},{6,7},{7,8},{8,9},{9,10},{10,1... | collective-permute-start | bytes 3145736 | tf_op jit(solution)/shard_map/ppermute | solution.py:22
  311.9 22.8 %collective-permute-start.13 = (bf16[256,2048]{0,1:T(8,128)(2,1)S(1)}, bf16[256,2048]{0,1:T(8,128)(2,1)S(1)}, u32[]{:S(2)}, u32[]{:S(2)}) collective-permute-start(bf16[256,2048]{0,1:T(8,128)(2,1)S(1)} %fusion.26), channel_id=1, source_target_pairs={{1,0},{2,1},{3,2},{4,3},{5,4},{6,5},{7,6},{8,7},{9,8},{10,9},{11,1... | collective-permute-start | bytes 3145736 | tf_op jit(solution)/shard_map/ppermute | solution.py:23
  362.0 26.0 %collective-permute-start.14 = (bf16[256,2048]{0,1:T(8,128)(2,1)S(1)}, bf16[256,2048]{0,1:T(8,128)(2,1)}, u32[]{:S(2)}, u32[]{:S(2)}) collective-permute-start(bf16[256,2048]{0,1:T(8,128)(2,1)S(1)} %fusion.29), channel_id=1, source_target_pairs={{0,1},{1,2},{2,3},{3,4},{4,5},{5,6},{6,7},{7,8},{8,9},{9,10},{10,1... | collective-permute-start | bytes 3145736 | tf_op jit(solution)/shard_map/ppermute | solution.py:22
  367.5 22.7 %collective-permute-start.15 = (bf16[256,2048]{0,1:T(8,128)(2,1)S(1)}, bf16[256,2048]{0,1:T(8,128)(2,1)S(1)}, u32[]{:S(2)}, u32[]{:S(2)}) collective-permute-start(bf16[256,2048]{0,1:T(8,128)(2,1)S(1)} %fusion.29), channel_id=1, source_target_pairs={{1,0},{2,1},{3,2},{4,3},{5,4},{6,5},{7,6},{8,7},{9,8},{10,9},{11,1... | collective-permute-start | bytes 3145736 | tf_op jit(solution)/shard_map/ppermute | solution.py:23
  440.4 195.0 %reduce-scatter.2.cloned.1.call-start = ((), (), s32[]{:S(2)}) async-start(), calls=%async_computation.4 | async-start | bytes 2359296 | tf_op jit(solution)/shard_map/reduce_scatter | solution.py:97
  440.4 29.0 %collective-permute-start.16 = (bf16[256,2048]{0,1:T(8,128)(2,1)S(1)}, bf16[256,2048]{0,1:T(8,128)(2,1)}, u32[]{:S(2)}, u32[]{:S(2)}) collective-permute-start(bf16[256,2048]{0,1:T(8,128)(2,1)S(1)} %fusion.32), channel_id=1, source_target_pairs={{0,1},{1,2},{2,3},{3,4},{4,5},{5,6},{6,7},{7,8},{8,9},{9,10},{10,1... | collective-permute-start | bytes 3145736 | tf_op jit(solution)/shard_map/ppermute | solution.py:22
  441.1 28.4 %collective-permute-start.17 = (bf16[256,2048]{0,1:T(8,128)(2,1)S(1)}, bf16[256,2048]{0,1:T(8,128)(2,1)}, u32[]{:S(2)}, u32[]{:S(2)}) collective-permute-start(bf16[256,2048]{0,1:T(8,128)(2,1)S(1)} %fusion.32), channel_id=1, source_target_pairs={{1,0},{2,1},{3,2},{4,3},{5,4},{6,5},{7,6},{8,7},{9,8},{10,9},{11,1... | collective-permute-start | bytes 3145736 | tf_op jit(solution)/shard_map/ppermute | solution.py:23
  485.0 103.2 %copy-start.5 = (bf16[16,256,128]{2,1,0:T(8,128)(2,1)S(1)}, bf16[16,256,128]{2,1,0:T(8,128)(2,1)}, u32[]{:S(2)}) copy-start(bf16[16,256,128]{2,1,0:T(8,128)(2,1)} %copy.54) | copy-start | bytes 3145732
  588.1 48.9 %copy-start.1 = (bf16[2,5,128,128]{3,2,1,0:T(8,128)(2,1)S(1)}, bf16[2,5,128,128]{3,2,1,0:T(8,128)(2,1)}, u32[]{:S(2)}) copy-start(bf16[2,5,128,128]{3,2,1,0:T(8,128)(2,1)} %param.7) | copy-start | bytes 983044
  (12 other events, 29.4 us)
Sparse Core Ops, SparseCore 0:
  440.5 147.6 all-gather.1
  598.0 37.2 reduce-scatter.1
where the time goes:
time: 654 us; the launch traced here: 644 us
  waiting for transfers between devices  272 us (42%)
  matrix products  118 us (18%)
  local copies, waits for them, and re-layouts  108 us (17%)
  blocking collectives  51 us (8%)
  starting transfers between devices  40.7 us (6%)
  other arithmetic  39.5 us (6%)
  between operations  14.6 us (2%)
    ppermute x9, waiting for transfers between devices, extended(): before = lax.ppermute(last, axis, up)  153 us
    dot_general x45, matrix products, apply_operator(): jnp.einsum('iab,ibm->iam', tiles[:, offset], window[offset:offset + local...  108 us
    all_gather x1, waiting for transfers between devices, body(): lax.all_gather(vec_part, 'col', axis=1, tiled=True)  73.5 us
    slice x24, local copies, waits for them, and re-layouts, apply_operator(): window[offset:offset + local_blocks]  47.2 us
    reduce_scatter x1, waiting for transfers between devices, body(): lax.psum_scatter(partial_terms, 'row', scatter_dimension=0, tiled=True)  37.4 us
    all_to_all x1, blocking collectives, body(): lax.all_to_all(applied, 'col', split_axis=1, concat_axis=0, tiled=True)  29.4 us
    reshape x8, local copies, waits for them, and re-layouts, apply_operator(): return summed.reshape(source.shape)  23.3 us
    ppermute x9, starting transfers between devices, extended(): after = lax.ppermute(initial, axis, down)  22.5 us
  transfers between devices with their start and end apart: 20, of which 15 were waited for; matrix products, arithmetic and copies ran while one was open for 8% of the time, Pallas kernels for 0%

commit v1 on v0

v1 whole, which is shorter than its diff:
```python
import functools
import math

import jax
import jax.numpy as jnp
from jax import lax
from jax.experimental import pallas as pl
from jax.experimental.pallas import tpu as pltpu
from jax.sharding import PartitionSpec as P

DEGREE = 8
MESH = pl.DeviceIdType.MESH

filter_center = 0.25
filter_half = 1.75


def band_tiles(blocks, block_cols, block_count, first_block, total_blocks):
    local_blocks = blocks.shape[0]
    slot_count = blocks.shape[1]
    reach_blocks = (slot_count - 1) // 2
    relative = jnp.mod(block_cols - first_block + reach_blocks, total_blocks)
    row_ids = jnp.arange(local_blocks, dtype=jnp.int32)
    slot_ids = jnp.arange(slot_count, dtype=jnp.int32)
    in_use = slot_ids[None, :] < block_count[:, None]
    matches = jnp.logical_and(
        relative[:, :, None] == row_ids[:, None, None] + slot_ids[None, None, :], in_use[:, :, None]
    )
    selector = jnp.where(matches, 1.0, 0.0).astype(jnp.bfloat16)
    return jnp.einsum(
        "iko,ikab->ioab", selector, blocks, preferred_element_type=jnp.float32
    ).astype(jnp.bfloat16)


def filter_kernel(n_row, v_ref, h_ref, f_ref, a_ref, band, ext0, ext1, send_sem, recv_sem):
    rows = v_ref.shape[0]
    blk = h_ref.shape[2]
    edge = 2 * blk
    pairs = rows // edge
    me = lax.axis_index("row")
    up, down = lax.rem(me + 1, n_row), lax.rem(me + n_row - 1, n_row)

    barrier = pltpu.get_barrier_semaphore()
    for neighbour in (up, down):
        pl.semaphore_signal(barrier, inc=1, device_id={"row": neighbour}, device_id_type=MESH)
    pl.semaphore_wait(barrier, 2)

    ext = (ext0, ext1)

    def send(slot):
        copies = (
            pltpu.make_async_remote_copy(
                src_ref=ext[slot].at[pl.ds(rows, edge)],
                dst_ref=ext[slot].at[pl.ds(0, edge)],
                send_sem=send_sem.at[slot, 0],
                recv_sem=recv_sem.at[slot, 0],
                device_id={"row": up},
                device_id_type=MESH,
            ),
            pltpu.make_async_remote_copy(
                src_ref=ext[slot].at[pl.ds(edge, edge)],
                dst_ref=ext[slot].at[pl.ds(rows + edge, edge)],
                send_sem=send_sem.at[slot, 1],
                recv_sem=recv_sem.at[slot, 1],
                device_id={"row": down},
                device_id_type=MESH,
            ),
        )
        for copy in copies:
            copy.start()
        return copies

    ext0[pl.ds(edge, rows), :] = v_ref[...]
    copies = send(0)

    def build(j, carry):
        for half in range(2):
            i = 2 * j + half
            for offset in range(5):
                band[j, pl.ds(half * blk, blk), pl.ds((offset + half) * blk, blk)] = h_ref[i, offset]
            band[j, pl.ds(half * blk, blk), pl.ds((5 - 5 * half) * blk, blk)] = jnp.zeros(
                (blk, blk), jnp.bfloat16
            )
        return carry

    lax.fori_loop(0, pairs, build, 0)

    for step in range(DEGREE + 1):
        now, later = step % 2, (step + 1) % 2
        source, target = ext[now], ext[later]

        def pair(j, carry):
            base = pl.multiple_of(j * edge, edge)
            own = pl.ds(pl.multiple_of(base + edge, edge), edge)
            product = jnp.dot(
                band[j], source[pl.ds(base, 3 * edge), :], preferred_element_type=jnp.float32
            )
            if step == DEGREE:
                a_ref[pl.ds(base, edge), :] = product.astype(jnp.bfloat16)
                return carry
            shifted = product - filter_center * source[own, :].astype(jnp.float32)
            if step == 0:
                result = shifted / filter_half
            else:
                result = 2.0 * shifted / filter_half - target[own, :].astype(jnp.float32)
            result = result.astype(jnp.bfloat16)
            target[own, :] = result
            if step == DEGREE - 1:
                f_ref[pl.ds(base, edge), :] = result
            return carry

        lax.fori_loop(1, pairs - 1, pair, 0, unroll=2)
        for copy in copies:
            copy.wait()
        pair(0, 0)
        pair(pairs - 1, 0)
        if step < DEGREE:
            copies = send(later)


def chebyshev(vectors, tiles, n_row):
    rows, width = vectors.shape
    blk = tiles.shape[2]
    pairs = rows // (2 * blk)
    vmem = pl.BlockSpec(memory_space=pltpu.VMEM)
    return pl.pallas_call(
        functools.partial(filter_kernel, n_row),
        out_shape=[jax.ShapeDtypeStruct((rows, width), jnp.bfloat16)] * 2,
        in_specs=[vmem, vmem],
        out_specs=[vmem, vmem],
        scratch_shapes=[
            pltpu.VMEM((pairs, 2 * blk, 6 * blk), jnp.bfloat16),
            pltpu.VMEM((rows + 4 * blk, width), jnp.bfloat16),
            pltpu.VMEM((rows + 4 * blk, width), jnp.bfloat16),
            pltpu.SemaphoreType.DMA((2, 2)),
            pltpu.SemaphoreType.DMA((2, 2)),
        ],
        compiler_params=pltpu.CompilerParams(
            collective_id=0, has_side_effects=True, vmem_limit_bytes=40 * 1024 * 1024
        ),
    )(vectors, tiles)


def body(vectors, block_count, block_cols, blocks):
    n_row = lax.axis_size("row")
    n_col = lax.axis_size("col")
    local_blocks = blocks.shape[0]
    total_blocks = local_blocks * n_row * n_col
    first_block = lax.axis_index(("row", "col")) * local_blocks
    tiles = band_tiles(blocks, block_cols, block_count, first_block, total_blocks)
    row_scale = 1.0 / math.sqrt(vectors.shape[0] * n_row * n_col)
    width = vectors.shape[1] // n_col
    columns = lax.all_to_all(vectors, "col", split_axis=1, concat_axis=0, tiled=True)
    all_tiles = lax.all_gather(tiles, "col", axis=0, tiled=True)
    filtered, applied = chebyshev(columns, all_tiles, n_row)
    paired = jnp.concatenate([applied, filtered], axis=1)
    partial_terms = lax.dot_general(
        lax.all_gather(filtered, "col", axis=1, tiled=True),
        paired,
        (((0,), (0,)), ((), ())),
        preferred_element_type=jnp.float32,
    )
    summed = lax.psum_scatter(partial_terms, "row", scatter_dimension=0, tiled=True)
    hamiltonian_proj = summed[:, :width] * row_scale
    intersection_proj = summed[:, width:] * row_scale
    return (hamiltonian_proj, intersection_proj)


def solution(mesh):
    in_specs = (
        P(("row", "col"), None),
        P(("row", "col")),
        P(("row", "col"), None),
        P(("row", "col"), None, None, None),
    )
    out_specs = (P("row", "col"), P("row", "col"))
    return jax.shard_map(body, mesh=mesh, in_specs=in_specs, out_specs=out_specs, check_vma=False)
```

time: 654 us -> 287 us (0.44); the launches traced: 644 us -> 287 us
  local copies, waits for them, and re-layouts: 108 us -> 3.55 us
  matrix products: 118 us -> 13.6 us
  waiting for transfers between devices: 272 us -> 189 us
  starting transfers between devices: 40.7 us -> 0.3 us
  Pallas kernels: 0 us -> 37.5 us
  other arithmetic: 39.5 us -> 3.18 us
  blocking collectives: 51 us -> 25.9 us
    ppermute x18 -> x0, waiting for transfers between devices: 161 us -> none  [the longest x9 153 us: extended(): before = lax.ppermute(last, axis, up)]
    dot_general x46 -> x1, matrix products: 118 us -> 12.3 us  [body(): lax.dot_general(lax.all_gather(filtered, 'col', axis=1, tiled=True), pair...]
    all_gather x1 -> x2, waiting for transfers between devices: 73.5 us -> 154 us  [the longest x1 117 us: body(): lax.all_gather(filtered, 'col', axis=1, tiled=True)]
    slice x25 -> x0, local copies, waits for them, and re-layouts: 47.6 us -> none  [the longest x24 47.2 us: apply_operator(): window[offset:offset + local_blocks]]
    ppermute x18 -> x0, starting transfers between devices: 40.6 us -> none  [the longest x9 22.5 us: extended(): after = lax.ppermute(initial, axis, down)]
    pallas_call x0 -> x1, Pallas kernels: none -> 37.5 us  [chebyshev(): pl.pallas_call(functools.partial(filter_kernel, n_row), out_shape=[jax.Sh...]
    ppermute x16 -> x0, local copies, waits for them, and re-layouts: 30.3 us -> none  [the longest x8 18.1 us: extended(): before = lax.ppermute(last, axis, up)]
    all_to_all x2 -> x1, blocking collectives: 51 us -> 25.9 us  [body(): lax.all_to_all(vectors, 'col', split_axis=1, concat_axis=0, tiled=True)]
  transfers between devices with their start and end apart: 20 -> 3, of which waited for: 15 -> 3; matrix products, arithmetic and copies ran while one was open for 8% -> 0% of each run, Pallas kernels for 0% -> 0%
where the time goes in v1:
time: 287 us
  waiting for transfers between devices  189 us (66%)
  Pallas kernels  37.5 us (13%)
  blocking collectives  25.9 us (9%)
  between operations  13.8 us (5%)
  matrix products  13.6 us (5%)
  local copies, waits for them, and re-layouts  3.55 us (1%)
  other arithmetic  3.18 us (1%)
    all_gather x1, waiting for transfers between devices, body(): lax.all_gather(filtered, 'col', axis=1, tiled=True)  117 us
    pallas_call x1, Pallas kernels, chebyshev(): pl.pallas_call(functools.partial(filter_kernel, n_row), out_shape=[jax.Sh...  37.5 us
    all_gather x1, waiting for transfers between devices, body(): all_tiles = lax.all_gather(tiles, 'col', axis=0, tiled=True)  36.9 us
    reduce_scatter x1, waiting for transfers between devices, body(): lax.psum_scatter(partial_terms, 'row', scatter_dimension=0, tiled=True)  34.9 us
    all_to_all x1, blocking collectives, body(): lax.all_to_all(vectors, 'col', split_axis=1, concat_axis=0, tiled=True)  25.9 us
    dot_general x1, matrix products, body(): lax.dot_general(lax.all_gather(filtered, 'col', axis=1, tiled=True), pair...  12.3 us
  transfers between devices with their start and end apart: 3, of which 3 were waited for; matrix products, arithmetic and copies ran while one was open for 0% of the time, Pallas kernels for 0%

profile of v1, /device:TPU:16, one launch (start us, length us, event | category | flops | bytes accessed | tf_op | source)
XLA Modules:
  0.0 286.9 jit_solution(2217526072756495434)
XLA Ops:
  7.2 0.0 copy-start
  7.2 0.0 all-gather.3.cloned.1.call-start
  7.2 0.8 iota_compare_fusion
  8.0 0.7 and_select_fusion
  8.7 1.3 convolution_convert_fusion
  10.1 0.8 copy.11
  10.9 0.0 all-gather.3.cloned.1.call-update
  10.9 0.0 all-gather.5.cloned.1.call-start
  10.9 0.0 copy-done
  10.9 0.3 copy_bitcast_fusion
  11.2 25.9 %all_to_all.19 = bf16[256,16,128]{2,0,1:T(8,128)(2,1)S(1)} all-to-all(bf16[256,16,128]{2,0,1:T(8,128)(2,1)S(1)} %copy_bitcast_fusion), channel_id=1, replica_groups=mesh['row'=8,'col'=16] {'col'}, dimensions={1} | all-to-all | bytes 2097152 | tf_op jit(solution)/shard_map/all_to_all | solution.py:153
  37.1 36.9 %all-gather.3.cloned.1.call-done.h_ref = bf16[32,5,128,128]{3,2,1,0:T(8,128)(2,1)} async-done(((bf16[2,5,128,128]{3,2,1,0:T(8,128)(2,1)}), bf16[32,5,128,128]{3,2,1,0:T(8,128)(2,1)}) %all-gather.3.cloned.1.call-update) | async-done | bytes 5242896 | tf_op jit(solution)/shard_map/all_gather | solution.py:154
  74.0 0.0 copy-start.1
  74.0 2.5 copy-done.1
  76.5 37.5 %shard_map.59 = (bf16[4096,128]{1,0:T(8,128)(2,1)}, bf16[4096,128]{1,0:T(8,128)(2,1)S(1)}) custom-call(bf16[4096,128]{1,0:T(8,128)(2,1)S(1)} %bitcast.14, bf16[32,5,128,128]{3,2,1,0:T(8,128)(2,1)S(1)} %copy-done.1), custom_call_target="tpu_custom_call" | custom-call | tf_op jit(solution)/shard_map/pallas_call | solution.py:126
  114.0 0.0 all-gather.5.cloned.1.call-update
  114.0 0.2 reduce-scatter.2.cloned.1.call-start
  114.3 117.3 %all-gather.5.cloned.1.call-done = bf16[4096,2048]{1,0:T(8,128)(2,1)} async-done(((bf16[4096,128]{1,0:T(8,128)(2,1)}), bf16[4096,2048]{1,0:T(8,128)(2,1)}) %all-gather.5.cloned.1.call-update) | async-done | bytes 16777232 | tf_op jit(solution)/shard_map/all_gather | solution.py:158
  231.5 12.3 %fusion = f32[2048,256]{1,0:T(8,128)} fusion(bf16[4096,2048]{1,0:T(8,128)(2,1)} %all-gather.5.cloned.1.call-done, bf16[4096,128]{1,0:T(8,128)(2,1)} %get-tuple-element.4, bf16[4096,128]{1,0:T(8,128)(2,1)S(1)} %get-tuple-element.5), kind=kOutput, calls=%fused_computation | convolution fusion | flops 4299161600 | bytes 20971520 | tf_op jit(solution)/shard_map/dot_general | solution.py:157
  243.8 0.0 reduce-scatter.2.cloned.1.call-update
  243.8 34.9 %reduce-scatter.2.cloned.1.call-done = f32[256,256]{1,0:T(8,128)} async-done(((f32[2048,256]{1,0:T(8,128)}), f32[256,256]{1,0:T(8,128)}) %reduce-scatter.2.cloned.1.call-update) | async-done | bytes 262160 | tf_op jit(solution)/shard_map/reduce_scatter | solution.py:163
  278.7 1.7 slice_multiply_fusion
Async XLA Ops:
  7.2 3.8 %copy-start = (bf16[256,2048]{1,0:T(8,128)(2,1)S(1)}, bf16[256,2048]{1,0:T(8,128)(2,1)}, u32[]{:S(2)}) copy-start(bf16[256,2048]{1,0:T(8,128)(2,1)} %param.4) | copy-start | bytes 3145732
  7.2 66.8 %all-gather.3.cloned.1.call-start = ((), (), s32[]{:S(2)}) async-start(), calls=%async_computation.2 | async-start | bytes 5570560 | tf_op jit(solution)/shard_map/all_gather | solution.py:154
  10.9 220.6 %all-gather.5.cloned.1.call-start = ((), (), s32[]{:S(2)}) async-start(), calls=%async_computation.3 | async-start | bytes 17825792 | tf_op jit(solution)/shard_map/all_gather | solution.py:158
  74.0 2.5 copy-start.1
  114.0 164.7 %reduce-scatter.2.cloned.1.call-start = ((), (), s32[]{:S(2)}) async-start(), calls=%async_computation.4 | async-start | bytes 2359296 | tf_op jit(solution)/shard_map/reduce_scatter | solution.py:163
Sparse Core Ops, SparseCore 0:
  11.0 62.9 all-gather.2
  114.1 117.3 all-gather.4
  243.9 34.7 reduce-scatter.1

commit v2 on v1

--- a/solution.py
+++ b/solution.py
@@ -109,7 +109,7 @@
                 f_ref[pl.ds(base, edge), :] = result
             return carry
 
-        lax.fori_loop(1, pairs - 1, pair, 0, unroll=2)
+        lax.fori_loop(1, pairs - 1, pair, 0, unroll=7)
         for copy in copies:
             copy.wait()
         pair(0, 0)
@@ -141,6 +141,203 @@
     )(vectors, tiles)
 
 
+def project_kernel(scale, f_ref, a_ref, h_out, g_out, fown, aown, ft, away, keep, core_in, share, x_in, done, fin,
+                   fx_s, fx_r, ax_s, ax_r, up_s, up_r, dn_s, dn_r, core_s, core_r, x_s, x_r, z_s, z_r):
+    part = f_ref.shape[0] // 4
+    width = f_ref.shape[1]
+    half = 2 * width
+    row, col = lax.axis_index("row"), lax.axis_index("col")
+    z, k, y, x = row // 2, row % 2, col // 4, col % 4
+
+    def on_x(d):
+        return {"col": y * 4 + (x + d) % 4}
+
+    def on_y(d):
+        return {"col": ((y + d) % 4) * 4 + x}
+
+    def on_z(d):
+        return {"row": ((z + d) % 4) * 2 + k}
+
+    partner = {"row": z * 2 + 1 - k}
+
+    def remote(src, dst, send, recv, device):
+        return pltpu.make_async_remote_copy(
+            src_ref=src, dst_ref=dst, send_sem=send, recv_sem=recv, device_id=device, device_id_type=MESH
+        )
+
+    barrier = pltpu.get_barrier_semaphore()
+    for device in [on_x(1), on_x(2), on_x(3), on_y(1), on_y(3), on_z(1), on_z(2), on_z(3), partner]:
+        pl.semaphore_signal(barrier, inc=1, device_id=device, device_id_type=MESH)
+    pl.semaphore_wait(barrier, 9)
+
+    def lanes(i):
+        return pl.ds(pl.multiple_of(i * width, width), width)
+
+    def x_copy(src, dst, sems, d):
+        rows = pl.ds(pl.multiple_of(((x + d) % 4) * part, part), part)
+        return remote(src.at[rows], dst.at[:, lanes(x)], sems[0].at[d - 1], sems[1].at[d - 1], on_x(d))
+
+    f_copies = {d: x_copy(f_ref, fown, (fx_s, fx_r), d) for d in (1, 2, 3)}
+    a_copies = {d: x_copy(a_ref, aown, (ax_s, ax_r), d) for d in (1, 2, 3)}
+
+    def y_copy(from_slot, to_slot, d, index, up):
+        piece = pl.ds(pl.multiple_of(((x + d) % 4) * width, width), width)
+        sems = (up_s, up_r) if up else (dn_s, dn_r)
+        return remote(ft.at[from_slot, piece], ft.at[to_slot, piece], sems[0].at[index], sems[1].at[index],
+                      on_y(1 if up else 3))
+
+    own_up = [y_copy(0, 1, d, d, True) for d in range(4)]
+    own_dn = [y_copy(0, 2, d, d, False) for d in range(4)]
+    fwd_up = {0: y_copy(1, 3, 0, 4, True), 1: y_copy(1, 3, 1, 5, True)}
+    fwd_dn = {3: y_copy(2, 3, 3, 4, False), 2: y_copy(2, 3, 2, 5, False)}
+
+    def spread(d):
+        source = (x + d) % 4
+        piece = pl.ds(pl.multiple_of(source * width, width), width)
+        ft[0, piece, :] = fown[:, lanes(source)].T
+        own_up[d].start()
+        own_dn[d].start()
+
+    for d in (1, 3, 2):
+        f_copies[d].start()
+    mine = pl.ds(pl.multiple_of(x * part, part), part)
+    fown[:, lanes(x)] = f_ref[mine, :]
+    spread(0)
+    aown[:, lanes(x)] = a_ref[mine, :]
+    f_copies[1].wait_recv()
+    spread(3)
+    f_copies[3].wait_recv()
+    spread(1)
+    for d in (1, 3, 2):
+        a_copies[d].start()
+    own_up[0].wait_recv()
+    fwd_up[0].start()
+    f_copies[2].wait_recv()
+    spread(2)
+    own_up[1].wait_recv()
+    fwd_up[1].start()
+    own_dn[3].wait_recv()
+    fwd_dn[3].start()
+    own_dn[2].wait_recv()
+    fwd_dn[2].start()
+
+    core_copies = [remote(away.at[j], core_in.at[j], core_s.at[j], core_r.at[j], partner) for j in range(4)]
+    x_copies = [
+        [
+            remote(share.at[j, :, :, lanes((x + d) % 4)], x_in.at[j, d - 1], x_s.at[j, d - 1], x_r.at[j, d - 1], on_x(d))
+            for d in (1, 2, 3)
+        ]
+        for j in range(4)
+    ]
+
+    def tile(j):
+        for part_k, out in ((1 - k, away), (k, keep)):
+            lhs = ft[j, pl.ds(pl.multiple_of(part_k * half, half), half), :]
+            for m, rhs in enumerate((aown, fown)):
+                out[j, m] = jnp.dot(lhs, rhs[...], preferred_element_type=jnp.float32).astype(out.dtype)
+            if out is away:
+                core_copies[j].start()
+
+    def over_core(j):
+        core_copies[j].wait_recv()
+        share[j] = (keep[j] + core_in[j].astype(jnp.float32)).astype(jnp.bfloat16)
+        for copy in x_copies[j]:
+            copy.start()
+
+    def z_copy(j):
+        d = (y + (0, 3, 1, 2)[j] - z + 4) % 4
+        return d, remote(done.at[j], fin.at[d], z_s.at[j], z_r.at[d], on_z(d))
+
+    def over_x(j):
+        for copy in x_copies[j]:
+            copy.wait_recv()
+        total = share[j, :, :, lanes(x)].astype(jnp.float32)
+        for i in range(3):
+            total = total + x_in[j, i].astype(jnp.float32)
+        done[j] = total.astype(jnp.bfloat16)
+        d, copy = z_copy(j)
+
+        @pl.when(d != 0)
+        def _():
+            copy.start()
+
+        @pl.when(d == 0)
+        def _():
+            fin[0] = done[j]
+
+    for d in (1, 3, 2):
+        a_copies[d].wait_recv()
+    tile(0)
+    own_up[2].wait_recv()
+    own_up[3].wait_recv()
+    tile(1)
+    over_core(0)
+    own_dn[0].wait_recv()
+    own_dn[1].wait_recv()
+    tile(2)
+    over_core(1)
+    over_x(0)
+    over_core(2)
+    for copy in (*fwd_up.values(), *fwd_dn.values()):
+        copy.wait_recv()
+    tile(3)
+    over_x(1)
+    over_core(3)
+    over_x(2)
+    over_x(3)
+
+    for d in (1, 2, 3):
+        remote(done.at[0], fin.at[d], z_s.at[0], z_r.at[d], on_z(d)).wait_recv()
+    total = fin[0].astype(jnp.float32)
+    for d in (1, 2, 3):
+        total = total + fin[d].astype(jnp.float32)
+    h_out[...] = total[0] * scale
+    g_out[...] = total[1] * scale
+
+    for copy in (*f_copies.values(), *a_copies.values(), *own_up, *own_dn, *fwd_up.values(), *fwd_dn.values(),
+                 *core_copies, *(c for cs in x_copies for c in cs)):
+        copy.wait_send()
+    for j in range(4):
+        d, copy = z_copy(j)
+
+        @pl.when(d != 0)
+        def _():
+            copy.wait_send()
+
+
+def project(filtered, applied, scale):
+    rows, width = filtered.shape
+    part = rows // 4
+    wide, half = 4 * width, 2 * width
+    vmem = pl.BlockSpec(memory_space=pltpu.VMEM)
+    bf16 = jnp.bfloat16
+    dma = pltpu.SemaphoreType.DMA
+    return pl.pallas_call(
+        functools.partial(project_kernel, scale),
+        out_shape=[jax.ShapeDtypeStruct((half, width), jnp.float32)] * 2,
+        in_specs=[vmem, vmem],
+        out_specs=[vmem, vmem],
+        scratch_shapes=[
+            pltpu.VMEM((part, wide), bf16),
+            pltpu.VMEM((part, wide), bf16),
+            pltpu.VMEM((4, wide, part), bf16),
+            pltpu.VMEM((4, 2, half, wide), bf16),
+            pltpu.VMEM((4, 2, half, wide), jnp.float32),
+            pltpu.VMEM((4, 2, half, wide), bf16),
+            pltpu.VMEM((4, 2, half, wide), bf16),
+            pltpu.VMEM((4, 3, 2, half, width), bf16),
+            pltpu.VMEM((4, 2, half, width), bf16),
+            pltpu.VMEM((4, 2, half, width), bf16),
+            dma((3,)), dma((3,)), dma((3,)), dma((3,)),
+            dma((6,)), dma((6,)), dma((6,)), dma((6,)),
+            dma((4,)), dma((4,)), dma((4, 3)), dma((4, 3)), dma((4,)), dma((4,)),
+        ],
+        compiler_params=pltpu.CompilerParams(
+            collective_id=1, has_side_effects=True, vmem_limit_bytes=48 * 1024 * 1024
+        ),
+    )(filtered, applied)
+
+
 def body(vectors, block_count, block_cols, blocks):
     n_row = lax.axis_size("row")
     n_col = lax.axis_size("col")
@@ -149,20 +346,10 @@
     first_block = lax.axis_index(("row", "col")) * local_blocks
     tiles = band_tiles(blocks, block_cols, block_count, first_block, total_blocks)
     row_scale = 1.0 / math.sqrt(vectors.shape[0] * n_row * n_col)
-    width = vectors.shape[1] // n_col
     columns = lax.all_to_all(vectors, "col", split_axis=1, concat_axis=0, tiled=True)
     all_tiles = lax.all_gather(tiles, "col", axis=0, tiled=True)
     filtered, applied = chebyshev(columns, all_tiles, n_row)
-    paired = jnp.concatenate([applied, filtered], axis=1)
-    partial_terms = lax.dot_general(
-        lax.all_gather(filtered, "col", axis=1, tiled=True),
-        paired,
-        (((0,), (0,)), ((), ())),
-        preferred_element_type=jnp.float32,
-    )
-    summed = lax.psum_scatter(partial_terms, "row", scatter_dimension=0, tiled=True)
-    hamiltonian_proj = summed[:, :width] * row_scale
-    intersection_proj = summed[:, width:] * row_scale
+    hamiltonian_proj, intersection_proj = project(filtered, applied, row_scale)
     return (hamiltonian_proj, intersection_proj)
 
 

time: 287 us -> 190 us (0.66)
  waiting for transfers between devices: 189 us -> 37 us
  Pallas kernels: 37.5 us -> 104 us
  matrix products: 13.6 us -> 1.33 us
    all_gather x1 -> x0, waiting for transfers between devices: 117 us -> none  [body(): lax.all_gather(filtered, 'col', axis=1, tiled=True)]
    pallas_call x0 -> x1, Pallas kernels: none -> 67.6 us  [project(): pl.pallas_call(functools.partial(project_kernel, scale), out_shape=[jax.S...]
    reduce_scatter x1 -> x0, waiting for transfers between devices: 34.9 us -> none  [body(): lax.psum_scatter(partial_terms, 'row', scatter_dimension=0, tiled=True)]
    dot_general x1 -> x0, matrix products: 12.3 us -> none  [body(): lax.dot_general(lax.all_gather(filtered, 'col', axis=1, tiled=True), pair...]
  transfers between devices with their start and end apart: 3 -> 1, of which waited for: 3 -> 1; matrix products, arithmetic and copies ran while one was open for 0% -> 0% of each run, Pallas kernels for 0% -> 0%
where the time goes in v2:
time: 190 us; the launch traced here: 188 us
  Pallas kernels  104 us (55%)
  waiting for transfers between devices  37 us (19%)
  blocking collectives  25.8 us (14%)
  between operations  14.1 us (7%)
  local copies, waits for them, and re-layouts  4.86 us (3%)
    pallas_call x1, Pallas kernels, project(): pl.pallas_call(functools.partial(project_kernel, scale), out_shape=[jax.S...  67.6 us
    all_gather x1, waiting for transfers between devices, body(): all_tiles = lax.all_gather(tiles, 'col', axis=0, tiled=True)  37 us
    pallas_call x1, Pallas kernels, chebyshev(): pl.pallas_call(functools.partial(filter_kernel, n_row), out_shape=[jax.Sh...  36.1 us
    all_to_all x1, blocking collectives, body(): lax.all_to_all(vectors, 'col', split_axis=1, concat_axis=0, tiled=True)  25.8 us
    unnamed x6, local copies, waits for them, and re-layouts  3.81 us
  transfers between devices with their start and end apart: 1, of which 1 were waited for; matrix products, arithmetic and copies ran while one was open for 0% of the time, Pallas kernels for 0%

profile of v2, /device:TPU:16, one launch (start us, length us, event | category | flops | bytes accessed | tf_op | source)
XLA Modules:
  0.0 188.3 jit_solution(18365173064468109943)
XLA Ops:
  7.2 0.0 copy-start
  7.2 0.0 all-gather.2.cloned.1.call-start
  7.2 0.8 iota_compare_fusion
  8.0 0.7 and_select_fusion
  8.7 1.3 convolution_convert_fusion
  10.1 0.8 copy.11
  10.9 0.0 all-gather.2.cloned.1.call-update
  10.9 0.0 copy-done
  10.9 0.3 copy_bitcast_fusion
  11.2 25.8 %all_to_all.19 = bf16[256,16,128]{2,0,1:T(8,128)(2,1)S(1)} all-to-all(bf16[256,16,128]{2,0,1:T(8,128)(2,1)S(1)} %copy_bitcast_fusion), channel_id=1, replica_groups=mesh['row'=8,'col'=16] {'col'}, dimensions={1} | all-to-all | bytes 2097152 | tf_op jit(solution)/shard_map/all_to_all | solution.py:349
  37.0 37.0 %all-gather.2.cloned.1.call-done.h_ref = bf16[32,5,128,128]{3,2,1,0:T(8,128)(2,1)} async-done(((bf16[2,5,128,128]{3,2,1,0:T(8,128)(2,1)}), bf16[32,5,128,128]{3,2,1,0:T(8,128)(2,1)}) %all-gather.2.cloned.1.call-update) | async-done | bytes 5242896 | tf_op jit(solution)/shard_map/all_gather | solution.py:350
  73.9 0.0 copy-start.1
  73.9 2.5 %copy-done.1 = bf16[32,5,128,128]{3,2,1,0:T(8,128)(2,1)S(1)} copy-done((bf16[32,5,128,128]{3,2,1,0:T(8,128)(2,1)S(1)}, bf16[32,5,128,128]{3,2,1,0:T(8,128)(2,1)}, u32[]{:S(2)}) %copy-start.1) | copy-done | bytes 5242904
  76.4 36.1 %shard_map.59 = (bf16[4096,128]{1,0:T(8,128)(2,1)S(1)}, bf16[4096,128]{1,0:T(8,128)(2,1)S(1)}) custom-call(bf16[4096,128]{1,0:T(8,128)(2,1)S(1)} %bitcast.13, bf16[32,5,128,128]{3,2,1,0:T(8,128)(2,1)S(1)} %copy-done.1), custom_call_target="tpu_custom_call" | custom-call | tf_op jit(solution)/shard_map/pallas_call | solution.py:126
  112.5 67.6 %shard_map.60 = (f32[256,128]{1,0:T(8,128)S(1)}, f32[256,128]{1,0:T(8,128)S(1)}) custom-call(bf16[4096,128]{1,0:T(8,128)(2,1)S(1)} %get-tuple-element.4.f_ref, bf16[4096,128]{1,0:T(8,128)(2,1)S(1)} %get-tuple-element.5.a_ref), custom_call_target="tpu_custom_call" | custom-call | tf_op jit(solution)/shard_map/pallas_call | solution.py:315
  180.2 0.7 copy.19
  180.8 0.7 copy.20
Async XLA Ops:
  7.2 3.7 %copy-start = (bf16[256,2048]{1,0:T(8,128)(2,1)S(1)}, bf16[256,2048]{1,0:T(8,128)(2,1)}, u32[]{:S(2)}) copy-start(bf16[256,2048]{1,0:T(8,128)(2,1)} %param.4) | copy-start | bytes 3145732
  7.2 66.8 %all-gather.2.cloned.1.call-start = ((), (), s32[]{:S(2)}) async-start(), calls=%async_computation.1 | async-start | bytes 5570560 | tf_op jit(solution)/shard_map/all_gather | solution.py:350
  73.9 2.5 %copy-start.1 = (bf16[32,5,128,128]{3,2,1,0:T(8,128)(2,1)S(1)}, bf16[32,5,128,128]{3,2,1,0:T(8,128)(2,1)}, u32[]{:S(2)}) copy-start(bf16[32,5,128,128]{3,2,1,0:T(8,128)(2,1)} %all-gather.2.cloned.1.call-done.h_ref) | copy-start | bytes 15728644
Sparse Core Ops, SparseCore 0:
  11.0 62.8 all-gather.1

commit v3 on v2

--- a/solution.py
+++ b/solution.py
@@ -15,130 +15,249 @@
 filter_half = 1.75
 
 
-def band_tiles(blocks, block_cols, block_count, first_block, total_blocks):
-    local_blocks = blocks.shape[0]
-    slot_count = blocks.shape[1]
-    reach_blocks = (slot_count - 1) // 2
-    relative = jnp.mod(block_cols - first_block + reach_blocks, total_blocks)
-    row_ids = jnp.arange(local_blocks, dtype=jnp.int32)
-    slot_ids = jnp.arange(slot_count, dtype=jnp.int32)
-    in_use = slot_ids[None, :] < block_count[:, None]
-    matches = jnp.logical_and(
-        relative[:, :, None] == row_ids[:, None, None] + slot_ids[None, None, :], in_use[:, :, None]
-    )
-    selector = jnp.where(matches, 1.0, 0.0).astype(jnp.bfloat16)
-    return jnp.einsum(
-        "iko,ikab->ioab", selector, blocks, preferred_element_type=jnp.float32
-    ).astype(jnp.bfloat16)
-
-
-def filter_kernel(n_row, v_ref, h_ref, f_ref, a_ref, band, ext0, ext1, send_sem, recv_sem):
-    rows = v_ref.shape[0]
-    blk = h_ref.shape[2]
-    edge = 2 * blk
-    pairs = rows // edge
-    me = lax.axis_index("row")
-    up, down = lax.rem(me + 1, n_row), lax.rem(me + n_row - 1, n_row)
-
+def filter_kernel(n_row, total_blocks, cols_ref, count_ref, blocks_ref, v_ref, f_ref, a_ref,
+                  hg, band, ext0, ext1, halo, own_sem, v_s, v_r, h1_s, h1_r, h2_s, h2_r, e_s, e_r, halo_s, halo_r):
+    edge = v_ref.shape[0]
+    blk = edge // 2
+    pairs = 16
+    row, col = lax.axis_index("row"), lax.axis_index("col")
+    y, x = col // 4, col % 4
+    up, down = {"row": (row + 1) % n_row}, {"row": (row + n_row - 1) % n_row}
+
+    def place(dy, dx):
+        return ((y + dy) % 4) * 4 + (x + dx) % 4
+
+    def remote(src, dst, send, recv, device):
+        return pltpu.make_async_remote_copy(
+            src_ref=src, dst_ref=dst, send_sem=send, recv_sem=recv, device_id=device, device_id_type=MESH
+        )
+
+    others = [(dy, dx) for dy in range(4) for dx in range(4) if dy or dx]
     barrier = pltpu.get_barrier_semaphore()
-    for neighbour in (up, down):
-        pl.semaphore_signal(barrier, inc=1, device_id={"row": neighbour}, device_id_type=MESH)
-    pl.semaphore_wait(barrier, 2)
-
-    ext = (ext0, ext1)
-
-    def send(slot):
-        copies = (
-            pltpu.make_async_remote_copy(
-                src_ref=ext[slot].at[pl.ds(rows, edge)],
-                dst_ref=ext[slot].at[pl.ds(0, edge)],
-                send_sem=send_sem.at[slot, 0],
-                recv_sem=recv_sem.at[slot, 0],
-                device_id={"row": up},
-                device_id_type=MESH,
-            ),
-            pltpu.make_async_remote_copy(
-                src_ref=ext[slot].at[pl.ds(edge, edge)],
-                dst_ref=ext[slot].at[pl.ds(rows + edge, edge)],
-                send_sem=send_sem.at[slot, 1],
-                recv_sem=recv_sem.at[slot, 1],
-                device_id={"row": down},
-                device_id_type=MESH,
-            ),
+    for device in [up, down] + [{"col": place(dy, dx)} for dy, dx in others]:
+        pl.semaphore_signal(barrier, inc=1, device_id=device, device_id_type=MESH)
+
+    first = (row * pairs + col) * 2
+    for i in range(2):
+        for offset in range(3):
+            tile = jnp.zeros((blk, blk), jnp.bfloat16)
+            for slot in range(5):
+                relative = lax.rem(cols_ref[i, slot] - first - i + total_blocks, total_blocks)
+                hit = jnp.logical_and(relative == offset, slot < count_ref[i])
+                tile = jnp.where(hit, blocks_ref[i, slot], tile)
+            hg[col + 2, i, offset] = tile
+
+    pl.semaphore_wait(barrier, 17)
+
+    def lanes(i):
+        return pl.ds(pl.multiple_of(i * blk, blk), blk)
+
+    def rows_of(pair, count=1):
+        return pl.ds(pl.multiple_of((pair + 2) * edge, edge), count * edge)
+
+    def unit(h, a, b):
+        return hg.at[place(b, a) + 2 if h == 0 else place(a, b) + 2, h]
+
+    def tile_copy(h, a, b, to_a, to_b, send, recv):
+        target = place(to_b, to_a) if h == 0 else place(to_a, to_b)
+        return remote(unit(h, a, b), unit(h, a, b), send, recv, {"col": target})
+
+    stage1, stage2 = [], []
+    for h in range(2):
+        sign = 1 if h == 0 else 3
+        moves = [(0, 1), (0, 3), (4 - sign, sign)]
+        stage1.append([tile_copy(h, a, 0, to, 0, h1_s.at[h, n], h1_r.at[h, n]) for n, (a, to) in enumerate(moves)])
+        lists = []
+        for a in range(4):
+            sign = 1 if a < 2 else 3
+            moves = [(0, 1), (0, 3), (4 - sign, sign)]
+            lists.append([
+                tile_copy(h, a, b, 0, to, h2_s.at[h, a, n], h2_r.at[h, a, n]) for n, (b, to) in enumerate(moves)
+            ])
+        stage2.append(lists)
+
+    v_copies = [
+        remote(v_ref.at[:, lanes(place(dy, dx))], ext0.at[rows_of(col)], v_s.at[dy * 4 + dx], v_r.at[dy * 4 + dx],
+               {"col": place(dy, dx)})
+        for dy, dx in others
+    ]
+    own = pltpu.make_async_copy(v_ref.at[:, lanes(col)], ext0.at[rows_of(col)], own_sem)
+
+    def scatter(pair, h):
+        slot = pair + 2
+        for offset in range(3):
+            band[slot, pl.ds(h * blk, blk), pl.ds((2 + h + offset) * blk, blk)] = hg[slot, h, offset]
+        zero = jnp.zeros((blk, blk), jnp.bfloat16)
+        band[slot, pl.ds(h * blk, blk), pl.ds((5 - 5 * h) * blk, blk)] = zero
+        if h == 0:
+            band[slot, pl.ds(blk, blk), pl.ds(2 * blk, blk)] = hg[slot, 0, 1].T
+            band[slot + 1, pl.ds(0, blk), pl.ds(0, blk)] = hg[slot, 0, 2].T
+        else:
+            band[slot + 1, pl.ds(0, blk), pl.ds(blk, blk)] = hg[slot, 1, 1].T
+            band[slot + 1, pl.ds(blk, blk), pl.ds(blk, blk)] = hg[slot, 1, 2].T
+
+    def scatter_unit(h, a, b):
+        scatter(place(b, a) if h == 0 else place(a, b), h)
+
+    for h in range(2):
+        stage1[h][0].start()
+        stage1[h][1].start()
+    for h in range(2):
+        stage2[h][0][0].start()
+        stage2[h][0][1].start()
+    own.start()
+    for copy in v_copies:
+        copy.start()
+    for h in range(2):
+        scatter(col, h)
+    for h in range(2):
+        for n, a in ((0, 3), (1, 1)):
+            stage1[h][n].wait_recv()
+            if n == h:
+                stage1[h][2].start()
+            stage2[h][a][0].start()
+            stage2[h][a][1].start()
+    for h in range(2):
+        scatter_unit(h, 3, 0)
+        scatter_unit(h, 1, 0)
+    for h in range(2):
+        stage1[h][2].wait_recv()
+        stage2[h][2][0].start()
+        stage2[h][2][1].start()
+    for h in range(2):
+        scatter_unit(h, 2, 0)
+    for a in (0, 3, 1, 2):
+        for h in range(2):
+            for n in (0, 1):
+                stage2[h][a][n].wait_recv()
+                if n == (0 if a < 2 else 1):
+                    stage2[h][a][2].start()
+        for h in range(2):
+            scatter_unit(h, a, 3)
+            scatter_unit(h, a, 1)
+    for a in (0, 3, 1, 2):
+        for h in range(2):
+            stage2[h][a][2].wait_recv()
+    to_up = remote(hg.at[pl.ds(pairs, 2)], hg.at[pl.ds(0, 2)], e_s.at[0], e_r.at[0], up)
+    to_down = remote(hg.at[2], hg.at[pairs + 2], e_s.at[1], e_r.at[1], down)
+    to_up.start()
+    to_down.start()
+    own.wait()
+    for copy in v_copies:
+        copy.wait_recv()
+
+    def halo_copy(side, parity):
+        return remote(ext0.at[rows_of(0 if side == 0 else pairs - 2, 2)], halo.at[parity, side],
+                      halo_s.at[parity, side], halo_r.at[parity, side], down if side == 0 else up)
+
+    for side in range(2):
+        halo_copy(side, 0).start()
+    for a in (0, 3, 1, 2):
+        for h in range(2):
+            scatter_unit(h, a, 2)
+
+    def product(j, source):
+        return jnp.dot(
+            band[j + 2], source[pl.ds(pl.multiple_of((j + 1) * edge, edge), 3 * edge), :],
+            preferred_element_type=jnp.float32,
         )
-        for copy in copies:
-            copy.start()
-        return copies
-
-    ext0[pl.ds(edge, rows), :] = v_ref[...]
-    copies = send(0)
-
-    def build(j, carry):
-        for half in range(2):
-            i = 2 * j + half
-            for offset in range(5):
-                band[j, pl.ds(half * blk, blk), pl.ds((offset + half) * blk, blk)] = h_ref[i, offset]
-            band[j, pl.ds(half * blk, blk), pl.ds((5 - 5 * half) * blk, blk)] = jnp.zeros(
-                (blk, blk), jnp.bfloat16
-            )
+
+    def update(j, source, target, initial):
+        shifted = product(j, source) - filter_center * source[rows_of(j), :].astype(jnp.float32)
+        if initial:
+            result = shifted / filter_half
+        else:
+            result = 2.0 * shifted / filter_half - target[rows_of(j), :].astype(jnp.float32)
+        target[rows_of(j), :] = result.astype(jnp.bfloat16)
+
+    def sweep(low, high, source, target, initial):
+        def one(j, carry):
+            update(j, source, target, initial)
+            return carry
+
+        lax.fori_loop(low, high, one, 0, unroll=high - low)
+
+    def land(side, parity):
+        copy = halo_copy(side, parity)
+        copy.wait()
+        ext0[rows_of(pairs if side == 0 else -2, 2), :] = halo[parity, side]
+
+    def cycle(parity, initial):
+        sweep(1, pairs - 1, ext0, ext1, initial)
+        sweep(2, pairs - 2, ext1, ext0, False)
+        for side in range(2):
+            if initial:
+                if side == 0:
+                    to_up.wait_recv()
+                    to_down.wait_recv()
+                    for pair in (-2, -1, pairs):
+                        for h in range(2):
+                            scatter(pair, h)
+            land(1 - side, parity)
+            low = side == 0
+            for j in (-1, 0) if low else (pairs, pairs - 1):
+                update(j, ext0, ext1, initial)
+        for side in range(2):
+            low = side == 0
+            for j in (0, 1) if low else (pairs - 1, pairs - 2):
+                update(j, ext1, ext0, False)
+            halo_copy(side, 1 - parity).start()
+
+    cycle(0, True)
+
+    def loop(c, carry):
+        cycle(lax.rem(c, 2), False)
         return carry
 
-    lax.fori_loop(0, pairs, build, 0)
-
-    for step in range(DEGREE + 1):
-        now, later = step % 2, (step + 1) % 2
-        source, target = ext[now], ext[later]
-
-        def pair(j, carry):
-            base = pl.multiple_of(j * edge, edge)
-            own = pl.ds(pl.multiple_of(base + edge, edge), edge)
-            product = jnp.dot(
-                band[j], source[pl.ds(base, 3 * edge), :], preferred_element_type=jnp.float32
-            )
-            if step == DEGREE:
-                a_ref[pl.ds(base, edge), :] = product.astype(jnp.bfloat16)
-                return carry
-            shifted = product - filter_center * source[own, :].astype(jnp.float32)
-            if step == 0:
-                result = shifted / filter_half
-            else:
-                result = 2.0 * shifted / filter_half - target[own, :].astype(jnp.float32)
-            result = result.astype(jnp.bfloat16)
-            target[own, :] = result
-            if step == DEGREE - 1:
-                f_ref[pl.ds(base, edge), :] = result
-            return carry
-
-        lax.fori_loop(1, pairs - 1, pair, 0, unroll=7)
-        for copy in copies:
-            copy.wait()
-        pair(0, 0)
-        pair(pairs - 1, 0)
-        if step < DEGREE:
-            copies = send(later)
-
-
-def chebyshev(vectors, tiles, n_row):
-    rows, width = vectors.shape
-    blk = tiles.shape[2]
-    pairs = rows // (2 * blk)
+    lax.fori_loop(1, DEGREE // 2, loop, 0)
+    f_ref[...] = ext0[rows_of(0, pairs), :]
+
+    def apply(j, carry):
+        a_ref[pl.ds(pl.multiple_of(j * edge, edge), edge), :] = product(j, ext0).astype(jnp.bfloat16)
+        return carry
+
+    lax.fori_loop(1, pairs - 1, apply, 0, unroll=pairs - 2)
+    for side in range(2):
+        land(1 - side, (DEGREE // 2) % 2)
+        apply(0 if side == 0 else pairs - 1, 0)
+
+    to_up.wait_send()
+    to_down.wait_send()
+    for h in range(2):
+        for copy in (*stage1[h], *(c for copies in stage2[h] for c in copies)):
+            copy.wait_send()
+    for copy in v_copies:
+        copy.wait_send()
+
+
+def chebyshev(vectors, block_count, block_cols, blocks, n_row, n_col):
+    edge, columns = vectors.shape
+    blk = blocks.shape[2]
+    width = columns // n_col
+    rows = edge * n_col
+    pairs = n_col
+    smem = pl.BlockSpec(memory_space=pltpu.SMEM)
     vmem = pl.BlockSpec(memory_space=pltpu.VMEM)
+    bf16 = jnp.bfloat16
+    dma = pltpu.SemaphoreType.DMA
     return pl.pallas_call(
-        functools.partial(filter_kernel, n_row),
-        out_shape=[jax.ShapeDtypeStruct((rows, width), jnp.bfloat16)] * 2,
-        in_specs=[vmem, vmem],
+        functools.partial(filter_kernel, n_row, blocks.shape[0] * n_row * n_col),
+        out_shape=[jax.ShapeDtypeStruct((rows, width), bf16)] * 2,
+        in_specs=[smem, smem, vmem, pl.BlockSpec(memory_space=pl.ANY)],
         out_specs=[vmem, vmem],
         scratch_shapes=[
-            pltpu.VMEM((pairs, 2 * blk, 6 * blk), jnp.bfloat16),
-            pltpu.VMEM((rows + 4 * blk, width), jnp.bfloat16),
-            pltpu.VMEM((rows + 4 * blk, width), jnp.bfloat16),
-            pltpu.SemaphoreType.DMA((2, 2)),
-            pltpu.SemaphoreType.DMA((2, 2)),
+            pltpu.VMEM((pairs + 3, 2, 3, blk, blk), bf16),
+            pltpu.VMEM((pairs + 4, edge, 6 * blk), bf16),
+            pltpu.VMEM((rows + 4 * edge, width), bf16),
+            pltpu.VMEM((rows + 4 * edge, width), bf16),
+            pltpu.VMEM((2, 2, 2 * edge, width), bf16),
+            dma, dma((16,)), dma((16,)), dma((2, 3)), dma((2, 3)), dma((2, 4, 3)), dma((2, 4, 3)),
+            dma((2,)), dma((2,)), dma((2, 2)), dma((2, 2)),
         ],
         compiler_params=pltpu.CompilerParams(
-            collective_id=0, has_side_effects=True, vmem_limit_bytes=40 * 1024 * 1024
+            collective_id=0, has_side_effects=True, vmem_limit_bytes=48 * 1024 * 1024
         ),
-    )(vectors, tiles)
+    )(block_cols, block_count, blocks, vectors)
 
 
 def project_kernel(scale, f_ref, a_ref, h_out, g_out, fown, aown, ft, away, keep, core_in, share, x_in, done, fin,
@@ -341,14 +460,8 @@
 def body(vectors, block_count, block_cols, blocks):
     n_row = lax.axis_size("row")
     n_col = lax.axis_size("col")
-    local_blocks = blocks.shape[0]
-    total_blocks = local_blocks * n_row * n_col
-    first_block = lax.axis_index(("row", "col")) * local_blocks
-    tiles = band_tiles(blocks, block_cols, block_count, first_block, total_blocks)
     row_scale = 1.0 / math.sqrt(vectors.shape[0] * n_row * n_col)
-    columns = lax.all_to_all(vectors, "col", split_axis=1, concat_axis=0, tiled=True)
-    all_tiles = lax.all_gather(tiles, "col", axis=0, tiled=True)
-    filtered, applied = chebyshev(columns, all_tiles, n_row)
+    filtered, applied = chebyshev(vectors, block_count, block_cols, blocks, n_row, n_col)
     hamiltonian_proj, intersection_proj = project(filtered, applied, row_scale)
     return (hamiltonian_proj, intersection_proj)
 

time: 190 us -> 138 us (0.73)
  waiting for transfers between devices: 37 us -> 0 us
  Pallas kernels: 104 us -> 132 us
  blocking collectives: 25.8 us -> 0 us
  between operations: 14.1 us -> 0.66 us
    all_gather x1 -> x0, waiting for transfers between devices: 37 us -> none  [body(): all_tiles = lax.all_gather(tiles, 'col', axis=0, tiled=True)]
    pallas_call x1, Pallas kernels: 36.1 us -> 66.1 us  [chebyshev(): pl.pallas_call(functools.partial(filter_kernel, n_row, blocks.shape[0] *...]
    all_to_all x1 -> x0, blocking collectives: 25.8 us -> none  [body(): lax.all_to_all(vectors, 'col', split_axis=1, concat_axis=0, tiled=True)]
    pallas_call x1, Pallas kernels: 67.6 us -> 65.6 us  [project(): pl.pallas_call(functools.partial(project_kernel, scale), out_shape=[jax.S...]
    unnamed x6 -> x10, local copies, waits for them, and re-layouts: 3.81 us -> 4.84 us
  transfers between devices with their start and end apart: 1 -> 0, of which waited for: 1 -> 0; matrix products, arithmetic and copies ran while one was open for 0% -> 0% of each run, Pallas kernels for 0% -> 0%
where the time goes in v3:
time: 138 us; the launch traced here: 137 us
  Pallas kernels  132 us (96%)
  local copies, waits for them, and re-layouts  4.84 us (4%)
    pallas_call x1, Pallas kernels, chebyshev(): pl.pallas_call(functools.partial(filter_kernel, n_row, blocks.shape[0] *...  66.1 us
    pallas_call x1, Pallas kernels, project(): pl.pallas_call(functools.partial(project_kernel, scale), out_shape=[jax.S...  65.6 us
    unnamed x10, local copies, waits for them, and re-layouts  4.84 us

profile of v3, /device:TPU:16, one launch (start us, length us, event | category | flops | bytes accessed | tf_op | source)
XLA Modules:
  0.0 137.1 jit_solution(17215838196655308190)
XLA Ops:
  0.6 0.0 copy-start
  0.6 1.2 copy-done
  1.9 0.0 copy-start.1
  1.9 1.0 copy-done.1
  2.8 0.0 copy-start.2
  2.8 0.7 copy-done.2
  3.5 0.0 copy-start.3
  3.5 0.7 copy-done.3
  4.2 66.1 %shard_map.59 = (bf16[4096,128]{1,0:T(8,128)(2,1)S(1)}, bf16[4096,128]{1,0:T(8,128)(2,1)S(1)}) custom-call(s32[2,5]{1,0:T(2,128)S(1)} %copy-done.2, s32[2]{0:T(128)S(1)} %copy-done.3, bf16[2,5,128,128]{3,2,1,0:T(8,128)(2,1)S(1)} %copy-done.1, bf16[256,2048]{1,0:T(8,128)(2,1)S(1)} %copy-done), custom_call_target="tpu_custom_call" | custom-call | tf_op jit(solution)/shard_map/pallas_call | solution.py:243
  70.2 65.6 %shard_map.60 = (f32[256,128]{1,0:T(8,128)S(1)}, f32[256,128]{1,0:T(8,128)S(1)}) custom-call(bf16[4096,128]{1,0:T(8,128)(2,1)S(1)} %get-tuple-element.4.f_ref, bf16[4096,128]{1,0:T(8,128)(2,1)S(1)} %get-tuple-element.5.a_ref), custom_call_target="tpu_custom_call" | custom-call | tf_op jit(solution)/shard_map/pallas_call | solution.py:434
  135.8 0.7 copy.8
  136.5 0.7 copy.9
Async XLA Ops:
  0.6 1.2 copy-start
  1.9 1.0 copy-start.1
  2.8 0.7 copy-start.2
  3.5 0.7 copy-start.3

commit v4 on v3

v4 whole, which is shorter than its diff:
```python
import functools
import math

import jax
import jax.numpy as jnp
from jax import lax
from jax.experimental import pallas as pl
from jax.experimental.pallas import tpu as pltpu
from jax.sharding import PartitionSpec as P

DEGREE = 8
REACH_IN = DEGREE + 1
MESH = pl.DeviceIdType.MESH

filter_center = 0.25
filter_half = 1.75


def kernel(n_row, total_blocks, scale, cols_hbm, count_hbm, blocks_hbm, v_ref, h_out, g_out,
           cols_ref, count_ref, blocks_ref, hg, band, vland, ext0, ext1, ftx, ft, aown, fown,
           away, keep, core_in, share, x_in, done, fin,
           in_sem, v_s, v_r, vh_s, vh_r, h1_s, h1_r, h2_s, h2_r, eu_s, eu_r, ed_s, ed_r,
           fx_s, fx_r, lo_s, lo_r, hi_s, hi_r, up_s, up_r, dn_s, dn_r, core_s, core_r, x_s, x_r, z_s, z_r):
    edge = v_ref.shape[0]
    blk = edge // 2
    pairs = 16
    out = REACH_IN
    row, col = lax.axis_index("row"), lax.axis_index("col")
    z, k, y, x = row // 2, row % 2, col // 4, col % 4
    up, down = {"row": (row + 1) % n_row}, {"row": (row + n_row - 1) % n_row}
    partner = {"row": z * 2 + 1 - k}
    across = {"row": (row + n_row - 1 + 2 * k) % n_row}

    def place(dy, dx):
        return ((y + dy) % 4) * 4 + (x + dx) % 4

    def on_x(d):
        return {"col": place(0, d)}

    def on_y(d):
        return {"col": place(d, 0)}

    def on_z(d):
        return {"row": ((z + d) % 4) * 2 + k}

    def remote(src, dst, send, recv, device):
        return pltpu.make_async_remote_copy(
            src_ref=src, dst_ref=dst, send_sem=send, recv_sem=recv, device_id=device, device_id_type=MESH
        )

    def lanes(i, size, count=1):
        return pl.ds(pl.multiple_of(i * size, size), count * size)

    others = [(dy, dx) for dy in range(4) for dx in range(4) if dy or dx]
    barrier = pltpu.get_barrier_semaphore()
    for device in [partner, across, on_z(1), on_z(2), on_z(3)] + [{"col": place(dy, dx)} for dy, dx in others]:
        pl.semaphore_signal(barrier, inc=1, device_id=device, device_id_type=MESH)

    fetch = [
        pltpu.make_async_copy(cols_hbm, cols_ref, in_sem.at[0]),
        pltpu.make_async_copy(count_hbm, count_ref, in_sem.at[1]),
        pltpu.make_async_copy(blocks_hbm, blocks_ref, in_sem.at[2]),
        pltpu.make_async_copy(v_ref.at[:, lanes(col, blk)], vland.at[col + out], in_sem.at[3]),
    ]
    for copy in fetch:
        copy.start()
    for copy in fetch[:3]:
        copy.wait()

    first = (row * pairs + col) * 2
    for i in range(2):
        for offset in range(3):
            tile = jnp.zeros((blk, blk), jnp.bfloat16)
            for slot in range(5):
                relative = lax.rem(cols_ref[i, slot] - first - i + total_blocks, total_blocks)
                hit = jnp.logical_and(relative == offset, slot < count_ref[i])
                tile = jnp.where(hit, blocks_ref[i, slot], tile)
            hg[col + out, i, offset] = tile

    pl.semaphore_wait(barrier, 20)

    def where(h, a, b):
        return place(b, a) if h == 0 else place(a, b)

    def tile_copy(h, a, b, to_a, to_b, send, recv):
        unit = hg.at[where(h, a, b) + out, h]
        return remote(unit, unit, send, recv, {"col": where(h, to_a, to_b)})

    stage1, stage2 = [], []
    for h in range(2):
        sign = 1 if h == 0 else 3
        moves = [(0, 1), (0, 3), (4 - sign, sign)]
        stage1.append([tile_copy(h, a, 0, to, 0, h1_s.at[h, n], h1_r.at[h, n]) for n, (a, to) in enumerate(moves)])
        lists = []
        for a in range(4):
            sign = 1 if a < 2 else 3
            moves = [(0, 1), (0, 3), (4 - sign, sign)]
            lists.append([
                tile_copy(h, a, b, 0, to, h2_s.at[h, a, n], h2_r.at[h, a, n]) for n, (b, to) in enumerate(moves)
            ])
        stage2.append(lists)

    v_copies = [
        remote(v_ref.at[:, lanes(place(dy, dx), blk)], vland.at[col + out], v_s.at[dy * 4 + dx],
               v_r.at[dy * 4 + dx], {"col": place(dy, dx)})
        for dy, dx in others
    ]

    def tile_up(p, h):
        return remote(hg.at[p + out, h], hg.at[p + out - pairs, h], eu_s.at[p + out - pairs, h],
                      eu_r.at[p + out - pairs, h], up)

    def tile_down(p, h):
        return remote(hg.at[p + out, h], hg.at[p + out + pairs, h], ed_s.at[p, h], ed_r.at[p, h], down)

    def pass_on(h, a, b):
        p = where(h, a, b)

        @pl.when(p >= pairs - out)
        def _():
            tile_up(p, h).start()

        @pl.when(p < out - 1)
        def _():
            tile_down(p, h).start()

    v_up = remote(vland.at[pl.ds(pairs, out)], vland.at[pl.ds(0, out)], vh_s.at[0], vh_r.at[0], up)
    v_down = remote(vland.at[pl.ds(out, out)], vland.at[pl.ds(pairs + out, out)], vh_s.at[1], vh_r.at[1], down)

    def scatter(slot, h):
        def put(s, r, c, value):
            band[s, pl.ds(r * blk, blk), pl.ds(c * blk, blk)] = value

        put(slot, 2 + h, h, hg[slot, h, 0])
        put(slot, 3 + h, h, hg[slot, h, 1].T)
        put(slot, 4 + h, h, hg[slot, h, 2].T)
        put(slot, 5 - 5 * h, h, jnp.zeros((blk, blk), jnp.bfloat16))
        if h == 0:
            put(slot, 2, 1, hg[slot, 0, 1])
            put(slot + 1, 0, 0, hg[slot, 0, 2])
        else:
            put(slot + 1, 1, 0, hg[slot, 1, 1])
            put(slot + 1, 1, 1, hg[slot, 1, 2])

    def scatter_unit(h, a, b):
        scatter(where(h, a, b) + out, h)

    for h in range(2):
        stage1[h][0].start()
        stage1[h][1].start()
    for h in range(2):
        stage2[h][0][0].start()
        stage2[h][0][1].start()
    for copy in v_copies:
        copy.start()
    for h in range(2):
        pass_on(h, 0, 0)
        scatter_unit(h, 0, 0)
    for h in range(2):
        for n, a in ((0, 3), (1, 1)):
            stage1[h][n].wait_recv()
            if n == h:
                stage1[h][2].start()
            stage2[h][a][0].start()
            stage2[h][a][1].start()
            pass_on(h, a, 0)
    for h in range(2):
        scatter_unit(h, 3, 0)
        scatter_unit(h, 1, 0)
    for h in range(2):
        stage1[h][2].wait_recv()
        stage2[h][2][0].start()
        stage2[h][2][1].start()
        pass_on(h, 2, 0)
    for h in range(2):
        scatter_unit(h, 2, 0)

    def receive(a):
        for h in range(2):
            for n, b in ((0, 3), (1, 1)):
                stage2[h][a][n].wait_recv()
                if n == (0 if a < 2 else 1):
                    stage2[h][a][2].start()
                pass_on(h, a, b)
        for h in range(2):
            scatter_unit(h, a, 3)
            scatter_unit(h, a, 1)

    def turn(slot):
        ext0[:, lanes(slot, edge)] = vland[slot].T

    for a in (0, 3, 1):
        receive(a)
    fetch[3].wait()
    for copy in v_copies:
        copy.wait_recv()
    v_up.start()
    v_down.start()
    receive(2)
    for a in (0, 3, 1, 2):
        for h in range(2):
            stage2[h][a][2].wait_recv()
            pass_on(h, a, 2)
    for a in (0, 3, 1, 2):
        for h in range(2):
            scatter_unit(h, a, 2)

    def turn_all(low, high):
        def one(slot, carry):
            turn(slot)
            return carry

        lax.fori_loop(low, high, one, 0)

    turn_all(out, out + pairs)

    def sweep(step, low, high):
        source, target = (ext0, ext1) if step % 2 else (ext1, ext0)

        def one(j, carry):
            own = lanes(j + out, edge)
            product = jnp.dot(source[:, lanes(j + out - 1, edge, 3)], band[j + out], preferred_element_type=jnp.float32)
            shifted = product - filter_center * source[:, own].astype(jnp.float32)
            if step == 1:
                result = shifted / filter_half
            else:
                result = 2.0 * shifted / filter_half - target[:, own].astype(jnp.float32)
            target[:, own] = result.astype(jnp.bfloat16)
            return carry

        count = high - low
        lax.fori_loop(low, high, one, 0, unroll=count // 2 if count % 2 == 0 else count)

    sweep(1, 1, pairs - 1)
    sweep(2, 2, pairs - 2)
    v_up.wait_recv()
    v_down.wait_recv()
    turn_all(0, out)
    turn_all(pairs + out, pairs + 2 * out)
    for p in range(out):
        for h in range(2):
            tile_up(p + pairs - out, h).wait_recv()
    for p in range(out - 1):
        for h in range(2):
            tile_down(p, h).wait_recv()

    def scatter_all(low, high):
        def one(slot, carry):
            scatter(slot, 0)
            scatter(slot, 1)
            return carry

        lax.fori_loop(low, high, one, 0)

    scatter_all(0, out)
    scatter_all(pairs + out, pairs + 2 * out - 1)
    sweep(1, 1 - out, 1)
    sweep(1, pairs - 1, pairs + out - 1)
    sweep(2, 2 - out, 2)
    sweep(2, pairs - 2, pairs + out - 2)
    for step in range(3, DEGREE + 1):
        sweep(step, step - out, pairs + out - step)

    part = 4 * edge
    width = blk
    half = 2 * width

    def x_copy(d, first_pair, count, offset, sems):
        pair = 4 * ((x + d) % 4) + first_pair + out
        return remote(ext0.at[:, lanes(pair, edge, count)], ftx.at[lanes(x, width), pl.ds(offset, count * edge)],
                      sems[0].at[d - 1], sems[1].at[d - 1], on_x(d))

    f_copies = {d: x_copy(d, 0, 4, edge, (fx_s, fx_r)) for d in (1, 2, 3)}
    lo_copies = {d: x_copy(d, -1, 1, 0, (lo_s, lo_r)) for d in (1, 2, 3)}
    hi_copies = {d: x_copy(d, 4, 1, 5 * edge, (hi_s, hi_r)) for d in (1, 2, 3)}
    inner = pl.ds(edge, part)

    def y_copy(from_slot, to_slot, d, index, is_up):
        piece = lanes((x + d) % 4, width)
        sems = (up_s, up_r) if is_up else (dn_s, dn_r)
        src = ftx.at[piece, inner] if from_slot == 0 else ft.at[from_slot - 1, piece]
        return remote(src, ft.at[to_slot - 1, piece], sems[0].at[index], sems[1].at[index], on_y(1 if is_up else 3))

    own_up = [y_copy(0, 1, d, d, True) for d in range(4)]
    own_dn = [y_copy(0, 2, d, d, False) for d in range(4)]
    fwd_up = {0: y_copy(1, 3, 0, 4, True), 1: y_copy(1, 3, 1, 5, True)}
    fwd_dn = {3: y_copy(2, 3, 3, 4, False), 2: y_copy(2, 3, 2, 5, False)}

    def spread(d):
        own_up[d].start()
        own_dn[d].start()

    for d in (1, 3, 2):
        f_copies[d].start()
    ftx[lanes(x, width), :] = ext0[:, lanes(4 * x - 1 + out, edge, 6)]
    spread(0)
    for d in (1, 3, 2):
        lo_copies[d].start()
        hi_copies[d].start()
    f_copies[1].wait_recv()
    spread(3)
    f_copies[3].wait_recv()
    spread(1)
    own_up[0].wait_recv()
    fwd_up[0].start()
    f_copies[2].wait_recv()
    spread(2)
    own_dn[3].wait_recv()
    fwd_dn[3].start()
    own_up[1].wait_recv()
    fwd_up[1].start()

    for d in (1, 3, 2):
        lo_copies[d].wait_recv()
        hi_copies[d].wait_recv()
    for q in range(4):
        rows = pl.ds(q * edge, edge)
        applied = jnp.dot(ftx[:, pl.ds(q * edge, 3 * edge)], band[4 * x + q + out], preferred_element_type=jnp.float32)
        aown[rows, :] = applied.astype(jnp.bfloat16).T
        fown[rows, :] = ftx[:, pl.ds((q + 1) * edge, edge)].T

    core_copies = [remote(away.at[j], core_in.at[j], core_s.at[j], core_r.at[j], partner) for j in range(4)]
    x_copies = [
        [
            remote(share.at[j, :, :, lanes((x + d) % 4, width)], x_in.at[j, d - 1], x_s.at[j, d - 1],
                   x_r.at[j, d - 1], on_x(d))
            for d in (1, 2, 3)
        ]
        for j in range(4)
    ]

    def tile(j):
        for part_k, target in ((1 - k, away), (k, keep)):
            rows = lanes(part_k, half)
            lhs = ftx[rows, inner] if j == 0 else ft[j - 1, rows, :]
            for m, rhs in enumerate((aown, fown)):
                target[j, m] = jnp.dot(lhs, rhs[...], preferred_element_type=jnp.float32).astype(target.dtype)
            if target is away:
                core_copies[j].start()

    def over_core(j):
        core_copies[j].wait_recv()
        share[j] = (keep[j] + core_in[j].astype(jnp.float32)).astype(jnp.bfloat16)
        for copy in x_copies[j]:
            copy.start()

    def z_copy(j):
        d = (y + (0, 3, 1, 2)[j] - z + 4) % 4
        return d, remote(done.at[j], fin.at[d], z_s.at[j], z_r.at[d], on_z(d))

    def over_x(j):
        for copy in x_copies[j]:
            copy.wait_recv()
        total = share[j, :, :, lanes(x, width)].astype(jnp.float32)
        for i in range(3):
            total = total + x_in[j, i].astype(jnp.float32)
        done[j] = total.astype(jnp.bfloat16)
        d, copy = z_copy(j)

        @pl.when(d != 0)
        def _():
            copy.start()

        @pl.when(d == 0)
        def _():
            fin[0] = done[j]

    tile(0)
    own_dn[2].wait_recv()
    fwd_dn[2].start()
    own_up[2].wait_recv()
    own_up[3].wait_recv()
    tile(1)
    over_core(0)
    own_dn[0].wait_recv()
    own_dn[1].wait_recv()
    tile(2)
    over_core(1)
    over_x(0)
    over_core(2)
    for copy in (*fwd_up.values(), *fwd_dn.values()):
        copy.wait_recv()
    tile(3)
    over_x(1)
    over_core(3)
    over_x(2)
    over_x(3)

    for d in (1, 2, 3):
        remote(done.at[0], fin.at[d], z_s.at[0], z_r.at[d], on_z(d)).wait_recv()
    total = fin[0].astype(jnp.float32)
    for d in (1, 2, 3):
        total = total + fin[d].astype(jnp.float32)
    h_out[...] = total[0] * scale
    g_out[...] = total[1] * scale

    for h in range(2):
        for copy in (*stage1[h], *(c for copies in stage2[h] for c in copies)):
            copy.wait_send()
        for p in range(out):
            tile_up(p + pairs - out, h).wait_send()
        for p in range(out - 1):
            tile_down(p, h).wait_send()
    for copy in (*v_copies, v_up, v_down, *f_copies.values(), *lo_copies.values(), *hi_copies.values(), *own_up,
                 *own_dn, *fwd_up.values(), *fwd_dn.values(), *core_copies, *(c for cs in x_copies for c in cs)):
        copy.wait_send()
    for j in range(4):
        d, copy = z_copy(j)

        @pl.when(d != 0)
        def _():
            copy.wait_send()


def body(vectors, block_count, block_cols, blocks):
    n_row = lax.axis_size("row")
    n_col = lax.axis_size("col")
    edge, columns = vectors.shape
    local_blocks, slots, blk, _ = blocks.shape
    width = columns // n_col
    scale = 1.0 / math.sqrt(edge * n_row * n_col)
    wide, half, part = 4 * width, 2 * width, 4 * edge
    reach = n_col + 2 * REACH_IN
    anywhere = pl.BlockSpec(memory_space=pl.ANY)
    vmem = pl.BlockSpec(memory_space=pltpu.VMEM)
    bf16 = jnp.bfloat16
    dma = pltpu.SemaphoreType.DMA
    return pl.pallas_call(
        functools.partial(kernel, n_row, local_blocks * n_row * n_col, scale),
        out_shape=[jax.ShapeDtypeStruct((half, width), jnp.float32)] * 2,
        in_specs=[anywhere] * 4,
        out_specs=[vmem, vmem],
        scratch_shapes=[
            pltpu.SMEM(block_cols.shape, jnp.int32),
            pltpu.SMEM(block_count.shape, jnp.int32),
            pltpu.VMEM(blocks.shape, bf16),
            pltpu.VMEM((reach - 1, 2, 3, blk, blk), bf16),
            pltpu.VMEM((reach, 6 * blk, edge), bf16),
            pltpu.VMEM((reach, edge, width), bf16),
            pltpu.VMEM((width, reach * edge), bf16),
            pltpu.VMEM((width, reach * edge), bf16),
            pltpu.VMEM((wide, part + 2 * edge), bf16),
            pltpu.VMEM((3, wide, part), bf16),
            pltpu.VMEM((part, wide), bf16),
            pltpu.VMEM((part, wide), bf16),
            pltpu.VMEM((4, 2, half, wide), bf16),
            pltpu.VMEM((4, 2, half, wide), jnp.float32),
            pltpu.VMEM((4, 2, half, wide), bf16),
            pltpu.VMEM((4, 2, half, wide), bf16),
            pltpu.VMEM((4, 3, 2, half, width), bf16),
            pltpu.VMEM((4, 2, half, width), bf16),
            pltpu.VMEM((4, 2, half, width), bf16),
            dma((4,)),
            dma((16,)), dma((16,)), dma((2,)), dma((2,)),
            dma((2, 3)), dma((2, 3)), dma((2, 4, 3)), dma((2, 4, 3)),
            dma((REACH_IN, 2)), dma((REACH_IN, 2)), dma((REACH_IN - 1, 2)), dma((REACH_IN - 1, 2)),
            dma((3,)), dma((3,)), dma((3,)), dma((3,)), dma((3,)), dma((3,)),
            dma((6,)), dma((6,)), dma((6,)), dma((6,)),
            dma((4,)), dma((4,)), dma((4, 3)), dma((4, 3)), dma((4,)), dma((4,)),
        ],
        compiler_params=pltpu.CompilerParams(
            collective_id=0, has_side_effects=True, vmem_limit_bytes=58 * 1024 * 1024
        ),
    )(block_cols, block_count, blocks, vectors)


def solution(mesh):
    in_specs = (
        P(("row", "col"), None),
        P(("row", "col")),
        P(("row", "col"), None),
        P(("row", "col"), None, None, None),
    )
    out_specs = (P("row", "col"), P("row", "col"))
    return jax.shard_map(body, mesh=mesh, in_specs=in_specs, out_specs=out_specs, check_vma=False)
```

time: 138 us -> 136 us (0.986)
  local copies, waits for them, and re-layouts: 4.84 us -> 2.26 us
    unnamed x10 -> x4, local copies, waits for them, and re-layouts: 4.84 us -> 2.26 us
    pallas_call x2 -> x1, Pallas kernels: 132 us -> 132 us  [body(): pl.pallas_call(functools.partial(kernel, n_row, local_blocks * n_row * n_...]
where the time goes in v4:
time: 136 us; the launch traced here: 134 us
  Pallas kernels  132 us (97%)
  local copies, waits for them, and re-layouts  2.26 us (2%)
    pallas_call x1, Pallas kernels, body(): pl.pallas_call(functools.partial(kernel, n_row, local_blocks * n_row * n_...  132 us

profile of v4, /device:TPU:16, one launch (start us, length us, event | category | flops | bytes accessed | tf_op | source)
XLA Modules:
  0.0 134.5 jit_solution(8284079310024504961)
XLA Ops:
  0.6 131.6 %shard_map.59 = (f32[256,128]{1,0:T(8,128)}, f32[256,128]{1,0:T(8,128)}) custom-call(s32[2,5]{1,0:T(2,128)} %cols_hbm.1, s32[2]{0:T(128)} %count_hbm.1, bf16[2,5,128,128]{3,2,1,0:T(8,128)(2,1)} %blocks_hbm.1, bf16[256,2048]{1,0:T(8,128)(2,1)} %v_ref.1), custom_call_target="tpu_custom_call" | custom-call | tf_op jit(solution)/shard_map/pallas_call | solution.py:428
  132.2 0.0 copy-start
  132.2 1.6 %copy.8 = f32[256,128]{1,0:T(8,128)} copy(f32[256,128]{1,0:T(8,128)} %get-tuple-element.4) | data formatting | bytes 262144
  133.8 0.0 copy-done
  133.8 0.7 copy.9
Async XLA Ops:
  132.2 1.6 %copy-start = (f32[256,128]{1,0:T(8,128)S(1)}, f32[256,128]{1,0:T(8,128)}, u32[]{:S(2)}) copy-start(f32[256,128]{1,0:T(8,128)} %get-tuple-element.5) | copy-start | bytes 393220

commit v5 on v4

--- a/solution.py
+++ b/solution.py
@@ -16,7 +16,7 @@
 filter_half = 1.75
 
 
-def kernel(n_row, total_blocks, scale, cols_hbm, count_hbm, blocks_hbm, v_ref, h_out, g_out,
+def kernel(n_row, total_blocks, cols_hbm, count_hbm, blocks_hbm, v_ref, sums,
            cols_ref, count_ref, blocks_ref, hg, band, vland, ext0, ext1, ftx, ft, aown, fown,
            away, keep, core_in, share, x_in, done, fin,
            in_sem, v_s, v_r, vh_s, vh_r, h1_s, h1_r, h2_s, h2_r, eu_s, eu_r, ed_s, ed_r,
@@ -124,8 +124,27 @@
         def _():
             tile_down(p, h).start()
 
-    v_up = remote(vland.at[pl.ds(pairs, out)], vland.at[pl.ds(0, out)], vh_s.at[0], vh_r.at[0], up)
-    v_down = remote(vland.at[pl.ds(out, out)], vland.at[pl.ds(pairs + out, out)], vh_s.at[1], vh_r.at[1], down)
+    def vector_up(p):
+        return remote(vland.at[p + out], vland.at[p + out - pairs], vh_s.at[0, p + out - pairs],
+                      vh_r.at[0, p + out - pairs], up)
+
+    def vector_down(p):
+        return remote(vland.at[p + out], vland.at[p + out + pairs], vh_s.at[1, p], vh_r.at[1, p], down)
+
+    def pass_vector(dy, dx):
+        if dy or dx:
+            v_copies[others.index((dy, dx))].wait_recv()
+        else:
+            fetch[3].wait()
+        p = place(4 - dy, 4 - dx)
+
+        @pl.when(p >= pairs - out)
+        def _():
+            vector_up(p).start()
+
+        @pl.when(p < out)
+        def _():
+            vector_down(p).start()
 
     def scatter(slot, h):
         def put(s, r, c, value):
@@ -167,6 +186,8 @@
     for h in range(2):
         scatter_unit(h, 3, 0)
         scatter_unit(h, 1, 0)
+    for dy, dx in ((0, 0), (0, 1), (0, 3), (1, 0), (3, 0)):
+        pass_vector(dy, dx)
     for h in range(2):
         stage1[h][2].wait_recv()
         stage2[h][2][0].start()
@@ -189,14 +210,15 @@
     def turn(slot):
         ext0[:, lanes(slot, edge)] = vland[slot].T
 
-    for a in (0, 3, 1):
+    for a, moves in (
+        (0, ((1, 1), (1, 3), (3, 1), (3, 3))),
+        (3, ((0, 2), (2, 0), (1, 2), (2, 1))),
+        (1, ((3, 2), (2, 3), (2, 2))),
+        (2, ()),
+    ):
         receive(a)
-    fetch[3].wait()
-    for copy in v_copies:
-        copy.wait_recv()
-    v_up.start()
-    v_down.start()
-    receive(2)
+        for dy, dx in moves:
+            pass_vector(dy, dx)
     for a in (0, 3, 1, 2):
         for h in range(2):
             stage2[h][a][2].wait_recv()
@@ -214,110 +236,110 @@
 
     turn_all(out, out + pairs)
 
-    def sweep(step, low, high):
+    def update(step, j):
         source, target = (ext0, ext1) if step % 2 else (ext1, ext0)
-
-        def one(j, carry):
-            own = lanes(j + out, edge)
-            product = jnp.dot(source[:, lanes(j + out - 1, edge, 3)], band[j + out], preferred_element_type=jnp.float32)
-            shifted = product - filter_center * source[:, own].astype(jnp.float32)
-            if step == 1:
-                result = shifted / filter_half
-            else:
-                result = 2.0 * shifted / filter_half - target[:, own].astype(jnp.float32)
-            target[:, own] = result.astype(jnp.bfloat16)
+        own = lanes(j + out, edge)
+        product = jnp.dot(source[:, lanes(j + out - 1, edge, 3)], band[j + out], preferred_element_type=jnp.float32)
+        shifted = product - filter_center * source[:, own].astype(jnp.float32)
+        if step == 1:
+            result = shifted / filter_half
+        else:
+            result = 2.0 * shifted / filter_half - target[:, own].astype(jnp.float32)
+        target[:, own] = result.astype(jnp.bfloat16)
+
+    for step in range(1, DEGREE):
+        def inside(j, carry):
+            update(step, j)
             return carry
 
-        count = high - low
-        lax.fori_loop(low, high, one, 0, unroll=count // 2 if count % 2 == 0 else count)
-
-    sweep(1, 1, pairs - 1)
-    sweep(2, 2, pairs - 2)
-    v_up.wait_recv()
-    v_down.wait_recv()
-    turn_all(0, out)
-    turn_all(pairs + out, pairs + 2 * out)
+        lax.fori_loop(step, pairs - step, inside, 0, unroll=pairs // 2 - step)
+
+    for p in range(out):
+        vector_up(p + pairs - out).wait_recv()
+        turn(p)
+        vector_down(p).wait_recv()
+        turn(p + pairs + out)
     for p in range(out):
         for h in range(2):
             tile_up(p + pairs - out, h).wait_recv()
-    for p in range(out - 1):
-        for h in range(2):
-            tile_down(p, h).wait_recv()
-
-    def scatter_all(low, high):
-        def one(slot, carry):
-            scatter(slot, 0)
-            scatter(slot, 1)
+            scatter(p, h)
+            if p < out - 1:
+                tile_down(p, h).wait_recv()
+                scatter(p + pairs + out, h)
+
+    for step in range(1, DEGREE + 1):
+        def outside(i, carry):
+            update(step, step - out + i)
+            update(step, pairs - step + i)
             return carry
 
-        lax.fori_loop(low, high, one, 0)
-
-    scatter_all(0, out)
-    scatter_all(pairs + out, pairs + 2 * out - 1)
-    sweep(1, 1 - out, 1)
-    sweep(1, pairs - 1, pairs + out - 1)
-    sweep(2, 2 - out, 2)
-    sweep(2, pairs - 2, pairs + out - 2)
-    for step in range(3, DEGREE + 1):
-        sweep(step, step - out, pairs + out - step)
+        lax.fori_loop(0, out, outside, 0, unroll=3)
 
     part = 4 * edge
     width = blk
     half = 2 * width
 
-    def x_copy(d, first_pair, count, offset, sems):
-        pair = 4 * ((x + d) % 4) + first_pair + out
+    def mate(e):
+        return (x, x + 1 - 2 * (x % 2), (x + 2) % 4, 3 - x)[e]
+
+    def x_copy(e, first_pair, count, offset, sems):
+        pair = 4 * mate(e) + first_pair + out
         return remote(ext0.at[:, lanes(pair, edge, count)], ftx.at[lanes(x, width), pl.ds(offset, count * edge)],
-                      sems[0].at[d - 1], sems[1].at[d - 1], on_x(d))
-
-    f_copies = {d: x_copy(d, 0, 4, edge, (fx_s, fx_r)) for d in (1, 2, 3)}
-    lo_copies = {d: x_copy(d, -1, 1, 0, (lo_s, lo_r)) for d in (1, 2, 3)}
-    hi_copies = {d: x_copy(d, 4, 1, 5 * edge, (hi_s, hi_r)) for d in (1, 2, 3)}
+                      sems[0].at[e - 1], sems[1].at[e - 1], {"col": y * 4 + mate(e)})
+
+    f_copies = {e: x_copy(e, 0, 4, edge, (fx_s, fx_r)) for e in (1, 2, 3)}
+    lo_copies = {e: x_copy(e, -1, 1, 0, (lo_s, lo_r)) for e in (1, 2, 3)}
+    hi_copies = {e: x_copy(e, 4, 1, 5 * edge, (hi_s, hi_r)) for e in (1, 2, 3)}
     inner = pl.ds(edge, part)
 
-    def y_copy(from_slot, to_slot, d, index, is_up):
-        piece = lanes((x + d) % 4, width)
+    def y_copy(from_slot, to_slot, e, index, is_up):
+        piece = lanes(mate(e), width)
         sems = (up_s, up_r) if is_up else (dn_s, dn_r)
         src = ftx.at[piece, inner] if from_slot == 0 else ft.at[from_slot - 1, piece]
         return remote(src, ft.at[to_slot - 1, piece], sems[0].at[index], sems[1].at[index], on_y(1 if is_up else 3))
 
-    own_up = [y_copy(0, 1, d, d, True) for d in range(4)]
-    own_dn = [y_copy(0, 2, d, d, False) for d in range(4)]
-    fwd_up = {0: y_copy(1, 3, 0, 4, True), 1: y_copy(1, 3, 1, 5, True)}
-    fwd_dn = {3: y_copy(2, 3, 3, 4, False), 2: y_copy(2, 3, 2, 5, False)}
-
-    def spread(d):
-        own_up[d].start()
-        own_dn[d].start()
-
-    for d in (1, 3, 2):
-        f_copies[d].start()
+    own_up = [y_copy(0, 1, e, e, True) for e in range(4)]
+    own_dn = [y_copy(0, 2, e, e, False) for e in range(4)]
+    fwd_up = {0: y_copy(1, 3, 0, 4, True), 3: y_copy(1, 3, 3, 5, True)}
+    fwd_dn = {1: y_copy(2, 3, 1, 4, False), 2: y_copy(2, 3, 2, 5, False)}
+
+    def spread(e):
+        own_up[e].start()
+        own_dn[e].start()
+
+    for e in (1, 3, 2):
+        f_copies[e].start()
     ftx[lanes(x, width), :] = ext0[:, lanes(4 * x - 1 + out, edge, 6)]
     spread(0)
-    for d in (1, 3, 2):
-        lo_copies[d].start()
-        hi_copies[d].start()
     f_copies[1].wait_recv()
+    spread(1)
+    f_copies[3].wait_recv()
     spread(3)
-    f_copies[3].wait_recv()
-    spread(1)
     own_up[0].wait_recv()
     fwd_up[0].start()
     f_copies[2].wait_recv()
     spread(2)
-    own_dn[3].wait_recv()
-    fwd_dn[3].start()
-    own_up[1].wait_recv()
-    fwd_up[1].start()
-
-    for d in (1, 3, 2):
-        lo_copies[d].wait_recv()
-        hi_copies[d].wait_recv()
-    for q in range(4):
+    for e in (1, 3, 2):
+        lo_copies[e].start()
+        hi_copies[e].start()
+    own_dn[1].wait_recv()
+    fwd_dn[1].start()
+
+    def apply(q):
         rows = pl.ds(q * edge, edge)
         applied = jnp.dot(ftx[:, pl.ds(q * edge, 3 * edge)], band[4 * x + q + out], preferred_element_type=jnp.float32)
         aown[rows, :] = applied.astype(jnp.bfloat16).T
         fown[rows, :] = ftx[:, pl.ds((q + 1) * edge, edge)].T
+
+    apply(1)
+    apply(2)
+    own_up[3].wait_recv()
+    fwd_up[3].start()
+    for e in (1, 3, 2):
+        lo_copies[e].wait_recv()
+        hi_copies[e].wait_recv()
+    apply(0)
+    apply(3)
 
     core_copies = [remote(away.at[j], core_in.at[j], core_s.at[j], core_r.at[j], partner) for j in range(4)]
     x_copies = [
@@ -329,14 +351,26 @@
         for j in range(4)
     ]
 
+    def half_tile(j, g):
+        target_k = x // 2 if g == 0 else 1 - x // 2
+        rows = lanes(target_k, half)
+        lhs = ftx[rows, inner] if j == 0 else ft[j - 1, rows, :]
+        parts = [jnp.dot(lhs, rhs[...], preferred_element_type=jnp.float32) for rhs in (aown, fown)]
+
+        @pl.when(target_k == k)
+        def _():
+            for m in range(2):
+                keep[j, m] = parts[m]
+
+        @pl.when(target_k != k)
+        def _():
+            for m in range(2):
+                away[j, m] = parts[m].astype(jnp.bfloat16)
+            core_copies[j].start()
+
     def tile(j):
-        for part_k, target in ((1 - k, away), (k, keep)):
-            rows = lanes(part_k, half)
-            lhs = ftx[rows, inner] if j == 0 else ft[j - 1, rows, :]
-            for m, rhs in enumerate((aown, fown)):
-                target[j, m] = jnp.dot(lhs, rhs[...], preferred_element_type=jnp.float32).astype(target.dtype)
-            if target is away:
-                core_copies[j].start()
+        half_tile(j, 0)
+        half_tile(j, 1)
 
     def over_core(j):
         core_copies[j].wait_recv()
@@ -368,21 +402,33 @@
     tile(0)
     own_dn[2].wait_recv()
     fwd_dn[2].start()
+    own_up[1].wait_recv()
     own_up[2].wait_recv()
-    own_up[3].wait_recv()
     tile(1)
     over_core(0)
     own_dn[0].wait_recv()
-    own_dn[1].wait_recv()
+    own_dn[3].wait_recv()
     tile(2)
     over_core(1)
     over_x(0)
     over_core(2)
-    for copy in (*fwd_up.values(), *fwd_dn.values()):
-        copy.wait_recv()
-    tile(3)
+    fwd_up[0].wait_recv()
+    fwd_dn[1].wait_recv()
+    half_tile(3, 0)
+
+    @pl.when(x // 2 == k)
+    def _():
+        over_core(3)
+
     over_x(1)
-    over_core(3)
+    fwd_up[3].wait_recv()
+    fwd_dn[2].wait_recv()
+    half_tile(3, 1)
+
+    @pl.when(x // 2 != k)
+    def _():
+        over_core(3)
+
     over_x(2)
     over_x(3)
 
@@ -391,8 +437,7 @@
     total = fin[0].astype(jnp.float32)
     for d in (1, 2, 3):
         total = total + fin[d].astype(jnp.float32)
-    h_out[...] = total[0] * scale
-    g_out[...] = total[1] * scale
+    sums[...] = total
 
     for h in range(2):
         for copy in (*stage1[h], *(c for copies in stage2[h] for c in copies)):
@@ -401,7 +446,10 @@
             tile_up(p + pairs - out, h).wait_send()
         for p in range(out - 1):
             tile_down(p, h).wait_send()
-    for copy in (*v_copies, v_up, v_down, *f_copies.values(), *lo_copies.values(), *hi_copies.values(), *own_up,
+    for p in range(out):
+        vector_up(p + pairs - out).wait_send()
+        vector_down(p).wait_send()
+    for copy in (*v_copies, *f_copies.values(), *lo_copies.values(), *hi_copies.values(), *own_up,
                  *own_dn, *fwd_up.values(), *fwd_dn.values(), *core_copies, *(c for cs in x_copies for c in cs)):
         copy.wait_send()
     for j in range(4):
@@ -425,11 +473,11 @@
     vmem = pl.BlockSpec(memory_space=pltpu.VMEM)
     bf16 = jnp.bfloat16
     dma = pltpu.SemaphoreType.DMA
-    return pl.pallas_call(
-        functools.partial(kernel, n_row, local_blocks * n_row * n_col, scale),
-        out_shape=[jax.ShapeDtypeStruct((half, width), jnp.float32)] * 2,
+    sums = pl.pallas_call(
+        functools.partial(kernel, n_row, local_blocks * n_row * n_col),
+        out_shape=jax.ShapeDtypeStruct((2, half, width), jnp.float32),
         in_specs=[anywhere] * 4,
-        out_specs=[vmem, vmem],
+        out_specs=vmem,
         scratch_shapes=[
             pltpu.SMEM(block_cols.shape, jnp.int32),
             pltpu.SMEM(block_count.shape, jnp.int32),
@@ -451,7 +499,7 @@
             pltpu.VMEM((4, 2, half, width), bf16),
             pltpu.VMEM((4, 2, half, width), bf16),
             dma((4,)),
-            dma((16,)), dma((16,)), dma((2,)), dma((2,)),
+            dma((16,)), dma((16,)), dma((2, REACH_IN)), dma((2, REACH_IN)),
             dma((2, 3)), dma((2, 3)), dma((2, 4, 3)), dma((2, 4, 3)),
             dma((REACH_IN, 2)), dma((REACH_IN, 2)), dma((REACH_IN - 1, 2)), dma((REACH_IN - 1, 2)),
             dma((3,)), dma((3,)), dma((3,)), dma((3,)), dma((3,)), dma((3,)),
@@ -462,6 +510,7 @@
             collective_id=0, has_side_effects=True, vmem_limit_bytes=58 * 1024 * 1024
         ),
     )(block_cols, block_count, blocks, vectors)
+    return (sums[0] * scale, sums[1] * scale)
 
 
 def solution(mesh):

time: 136 us -> 136 us (level)
  the two profiles are of different devices: /device:TPU:16 before, /device:TPU:56 now
where the time goes in v5:
time: 136 us
  Pallas kernels  133 us (98%)
  other arithmetic  1.69 us (1%)
    pallas_call x1, Pallas kernels, body(): pl.pallas_call(functools.partial(kernel, n_row, local_blocks * n_row * n_...  133 us

profile of v5, /device:TPU:56, one launch (start us, length us, event | category | flops | bytes accessed | tf_op | source)
XLA Modules:
  0.0 135.6 jit_solution(6535754174158425078)
XLA Ops:
  0.6 133.3 %shard_map.59 = f32[2,256,128]{2,1,0:T(8,128)} custom-call(s32[2,5]{1,0:T(2,128)} %cols_hbm.1, s32[2]{0:T(128)} %count_hbm.1, bf16[2,5,128,128]{3,2,1,0:T(8,128)(2,1)} %blocks_hbm.1, bf16[256,2048]{1,0:T(8,128)(2,1)} %v_ref.1), custom_call_target="tpu_custom_call" | custom-call | tf_op jit(solution)/shard_map/pallas_call | solution.py:476
  133.9 1.7 %multiply_bitcast_fusion = (f32[256,128]{1,0:T(8,128)}, f32[256,128]{1,0:T(8,128)}) fusion(f32[2,256,128]{2,1,0:T(8,128)} %shard_map.59), kind=kLoop, calls=%fused_computation | loop fusion | flops 65536 | bytes 524288 | tf_op jit(solution)/shard_map/mul | solution.py:513

commit v6 on v5

--- a/solution.py
+++ b/solution.py
@@ -18,9 +18,10 @@
 
 def kernel(n_row, total_blocks, cols_hbm, count_hbm, blocks_hbm, v_ref, sums,
            cols_ref, count_ref, blocks_ref, hg, band, vland, ext0, ext1, ftx, ft, aown, fown,
-           away, keep, core_in, share, x_in, done, fin,
+           away, keep, core_in, share, x_in, done, fin, zin, ksum, kx_in,
            in_sem, v_s, v_r, vh_s, vh_r, h1_s, h1_r, h2_s, h2_r, eu_s, eu_r, ed_s, ed_r,
-           fx_s, fx_r, lo_s, lo_r, hi_s, hi_r, up_s, up_r, dn_s, dn_r, core_s, core_r, x_s, x_r, z_s, z_r):
+           fx_s, fx_r, lo_s, lo_r, hi_s, hi_r, up_s, up_r, dn_s, dn_r, core_s, core_r, x_s, x_r, z_s, z_r,
+           zk_s, zk_r, kx_s, kx_r):
     edge = v_ref.shape[0]
     blk = edge // 2
     pairs = 16
@@ -164,37 +165,50 @@
     def scatter_unit(h, a, b):
         scatter(where(h, a, b) + out, h)
 
-    for h in range(2):
-        stage1[h][0].start()
-        stage1[h][1].start()
-    for h in range(2):
-        stage2[h][0][0].start()
-        stage2[h][0][1].start()
-    for copy in v_copies:
-        copy.start()
-    for h in range(2):
-        pass_on(h, 0, 0)
-        scatter_unit(h, 0, 0)
-    for h in range(2):
-        for n, a in ((0, 3), (1, 1)):
-            stage1[h][n].wait_recv()
-            if n == h:
-                stage1[h][2].start()
-            stage2[h][a][0].start()
-            stage2[h][a][1].start()
-            pass_on(h, a, 0)
-    for h in range(2):
-        scatter_unit(h, 3, 0)
-        scatter_unit(h, 1, 0)
-    for dy, dx in ((0, 0), (0, 1), (0, 3), (1, 0), (3, 0)):
-        pass_vector(dy, dx)
-    for h in range(2):
-        stage1[h][2].wait_recv()
-        stage2[h][2][0].start()
-        stage2[h][2][1].start()
-        pass_on(h, 2, 0)
-    for h in range(2):
-        scatter_unit(h, 2, 0)
+    def start_first():
+        for h in range(2):
+            stage1[h][0].start()
+            stage1[h][1].start()
+
+    def start_own():
+        for h in range(2):
+            stage2[h][0][0].start()
+            stage2[h][0][1].start()
+
+    def start_vectors(moves):
+        for move in moves:
+            v_copies[others.index(move)].start()
+
+    def pass_vectors(moves):
+        for dy, dx in moves:
+            pass_vector(dy, dx)
+
+    def pass_own():
+        for h in range(2):
+            pass_on(h, 0, 0)
+            scatter_unit(h, 0, 0)
+
+    def take_first():
+        for h in range(2):
+            for n, a in ((0, 3), (1, 1)):
+                stage1[h][n].wait_recv()
+                if n == h:
+                    stage1[h][2].start()
+                stage2[h][a][0].start()
+                stage2[h][a][1].start()
+                pass_on(h, a, 0)
+        for h in range(2):
+            scatter_unit(h, 3, 0)
+            scatter_unit(h, 1, 0)
+
+    def take_far():
+        for h in range(2):
+            stage1[h][2].wait_recv()
+            stage2[h][2][0].start()
+            stage2[h][2][1].start()
+            pass_on(h, 2, 0)
+        for h in range(2):
+            scatter_unit(h, 2, 0)
 
     def receive(a):
         for h in range(2):
@@ -207,25 +221,39 @@
             scatter_unit(h, a, 3)
             scatter_unit(h, a, 1)
 
+    def receive_far(a):
+        for h in range(2):
+            stage2[h][a][2].wait_recv()
+            pass_on(h, a, 2)
+        for h in range(2):
+            scatter_unit(h, a, 2)
+
     def turn(slot):
         ext0[:, lanes(slot, edge)] = vland[slot].T
 
-    for a, moves in (
-        (0, ((1, 1), (1, 3), (3, 1), (3, 3))),
-        (3, ((0, 2), (2, 0), (1, 2), (2, 1))),
-        (1, ((3, 2), (2, 3), (2, 2))),
-        (2, ()),
-    ):
-        receive(a)
-        for dy, dx in moves:
-            pass_vector(dy, dx)
-    for a in (0, 3, 1, 2):
-        for h in range(2):
-            stage2[h][a][2].wait_recv()
-            pass_on(h, a, 2)
-    for a in (0, 3, 1, 2):
-        for h in range(2):
-            scatter_unit(h, a, 2)
+    near = [(0, 1), (0, 3), (1, 0), (3, 0)]
+    middle = [(1, 1), (1, 3), (3, 1), (3, 3), (0, 2), (2, 0)]
+    distant = [(1, 2), (3, 2), (2, 1), (2, 3), (2, 2)]
+
+    start_first()
+    start_own()
+    start_vectors(near)
+    pass_own()
+    take_first()
+    pass_vectors([(0, 0)] + near)
+    start_vectors(middle)
+    take_far()
+    receive(0)
+    pass_vectors(middle)
+    start_vectors(distant)
+    receive(3)
+    receive_far(0)
+    receive(1)
+    receive_far(3)
+    pass_vectors(distant)
+    receive(2)
+    receive_far(1)
+    receive_far(2)
 
     def turn_all(low, high):
         def one(slot, carry):
@@ -342,14 +370,31 @@
     apply(3)
 
     core_copies = [remote(away.at[j], core_in.at[j], core_s.at[j], core_r.at[j], partner) for j in range(4)]
-    x_copies = [
-        [
-            remote(share.at[j, :, :, lanes((x + d) % 4, width)], x_in.at[j, d - 1], x_s.at[j, d - 1],
-                   x_r.at[j, d - 1], on_x(d))
-            for d in (1, 2, 3)
-        ]
-        for j in range(4)
+    far = (y - z + 4) % 4 == 2
+
+    def sum_copy(j, d):
+        src, dst = share.at[j, :, :, lanes((x + d) % 4, width)], x_in.at[j, d - 1]
+        if j < 3:
+            src, dst = share.at[j, 1, :, lanes((x + d) % 4, width)], x_in.at[j, d - 1, 1]
+        return remote(src, dst, x_s.at[j, d - 1], x_r.at[j, d - 1], on_x(d))
+
+    x_copies = [[sum_copy(j, d) for d in (1, 2, 3)] for j in range(4)]
+    kx_copies = [
+        remote(ksum.at[:, lanes((x + d) % 4, width)], kx_in.at[d - 1], kx_s.at[d - 1], kx_r.at[d - 1], on_x(d))
+        for d in (1, 2, 3)
     ]
+
+    def to_owner(j):
+        return (y + (0, 3, 1, 2)[j] - z + 4) % 4
+
+    def z_copy(j):
+        d = to_owner(j)
+        src, dst = (done.at[j], fin.at[d]) if j == 3 else (done.at[j, 1], fin.at[d, 1])
+        return d, remote(src, dst, z_s.at[j], z_r.at[d], on_z(d))
+
+    def zk_copy(j):
+        d = to_owner(j)
+        return d, remote(share.at[j, 0], zin.at[d], zk_s.at[j], zk_r.at[d], on_z(d))
 
     def half_tile(j, g):
         target_k = x // 2 if g == 0 else 1 - x // 2
@@ -377,18 +422,25 @@
         share[j] = (keep[j] + core_in[j].astype(jnp.float32)).astype(jnp.bfloat16)
         for copy in x_copies[j]:
             copy.start()
-
-    def z_copy(j):
-        d = (y + (0, 3, 1, 2)[j] - z + 4) % 4
-        return d, remote(done.at[j], fin.at[d], z_s.at[j], z_r.at[d], on_z(d))
+        if j < 3:
+            d, copy = zk_copy(j)
+
+            @pl.when(d != 0)
+            def _():
+                copy.start()
+
+            @pl.when(d == 0)
+            def _():
+                zin[0] = share[j, 0]
 
     def over_x(j):
         for copy in x_copies[j]:
             copy.wait_recv()
-        total = share[j, :, :, lanes(x, width)].astype(jnp.float32)
-        for i in range(3):
-            total = total + x_in[j, i].astype(jnp.float32)
-        done[j] = total.astype(jnp.bfloat16)
+        for m in (0, 1) if j == 3 else (1,):
+            total = share[j, m, :, lanes(x, width)].astype(jnp.float32)
+            for i in range(3):
+                total = total + x_in[j, i, m].astype(jnp.float32)
+            done[j, m] = total.astype(jnp.bfloat16)
         d, copy = z_copy(j)
 
         @pl.when(d != 0)
@@ -397,7 +449,8 @@
 
         @pl.when(d == 0)
         def _():
-            fin[0] = done[j]
+            for m in (0, 1) if j == 3 else (1,):
+                fin[0, m] = done[j, m]
 
     tile(0)
     own_dn[2].wait_recv()
@@ -430,14 +483,41 @@
         over_core(3)
 
     over_x(2)
+
+    @pl.when(jnp.logical_not(far))
+    def _():
+        for d in (1, 2, 3):
+            remote(share.at[0, 0], zin.at[d], zk_s.at[0], zk_r.at[d], on_z(d)).wait_recv()
+        total = zin[0].astype(jnp.float32)
+        for d in (1, 2, 3):
+            total = total + zin[d].astype(jnp.float32)
+        ksum[...] = total.astype(jnp.bfloat16)
+        for copy in kx_copies:
+            copy.start()
+
     over_x(3)
 
-    for d in (1, 2, 3):
-        remote(done.at[0], fin.at[d], z_s.at[0], z_r.at[d], on_z(d)).wait_recv()
-    total = fin[0].astype(jnp.float32)
-    for d in (1, 2, 3):
-        total = total + fin[d].astype(jnp.float32)
-    sums[...] = total
+    def add_up(first, rest):
+        total = first.astype(jnp.float32)
+        for term in rest:
+            total = total + term.astype(jnp.float32)
+        return total
+
+    @pl.when(jnp.logical_not(far))
+    def _():
+        for d in (1, 2, 3):
+            remote(done.at[0, 1], fin.at[d, 1], z_s.at[0], z_r.at[d], on_z(d)).wait_recv()
+        for copy in kx_copies:
+            copy.wait_recv()
+        sums[0] = add_up(ksum[:, lanes(x, width)], [kx_in[i] for i in range(3)])
+
+    @pl.when(far)
+    def _():
+        for d in (1, 2, 3):
+            remote(done.at[3], fin.at[d], z_s.at[3], z_r.at[d], on_z(d)).wait_recv()
+        sums[0] = add_up(fin[0, 0], [fin[d, 0] for d in (1, 2, 3)])
+
+    sums[1] = add_up(fin[0, 1], [fin[d, 1] for d in (1, 2, 3)])
 
     for h in range(2):
         for copy in (*stage1[h], *(c for copies in stage2[h] for c in copies)):
@@ -453,10 +533,14 @@
                  *own_dn, *fwd_up.values(), *fwd_dn.values(), *core_copies, *(c for cs in x_copies for c in cs)):
         copy.wait_send()
     for j in range(4):
-        d, copy = z_copy(j)
-
-        @pl.when(d != 0)
-        def _():
+        for d, copy in [z_copy(j)] + ([zk_copy(j)] if j < 3 else []):
+            @pl.when(d != 0)
+            def _():
+                copy.wait_send()
+
+    @pl.when(jnp.logical_not(far))
+    def _():
+        for copy in kx_copies:
             copy.wait_send()
 
 
@@ -498,6 +582,9 @@
             pltpu.VMEM((4, 3, 2, half, width), bf16),
             pltpu.VMEM((4, 2, half, width), bf16),
             pltpu.VMEM((4, 2, half, width), bf16),
+            pltpu.VMEM((4, half, wide), bf16),
+            pltpu.VMEM((half, wide), bf16),
+            pltpu.VMEM((3, half, width), bf16),
             dma((4,)),
             dma((16,)), dma((16,)), dma((2, REACH_IN)), dma((2, REACH_IN)),
             dma((2, 3)), dma((2, 3)), dma((2, 4, 3)), dma((2, 4, 3)),
@@ -505,6 +592,7 @@
             dma((3,)), dma((3,)), dma((3,)), dma((3,)), dma((3,)), dma((3,)),
             dma((6,)), dma((6,)), dma((6,)), dma((6,)),
             dma((4,)), dma((4,)), dma((4, 3)), dma((4, 3)), dma((4,)), dma((4,)),
+            dma((3,)), dma((4,)), dma((3,)), dma((3,)),
         ],
         compiler_params=pltpu.CompilerParams(
             collective_id=0, has_side_effects=True, vmem_limit_bytes=58 * 1024 * 1024

time: 136 us -> 129 us (0.949)
  the two profiles are of different devices: /device:TPU:56 before, /device:TPU:16 now
where the time goes in v6:
time: 129 us; the launch traced here: 126 us
  Pallas kernels  124 us (96%)
  other arithmetic  1.69 us (1%)
    pallas_call x1, Pallas kernels, body(): pl.pallas_call(functools.partial(kernel, n_row, local_blocks * n_row * n_...  124 us

profile of v6, /device:TPU:16, one launch (start us, length us, event | category | flops | bytes accessed | tf_op | source)
XLA Modules:
  0.0 126.4 jit_solution(4414459084772330719)
XLA Ops:
  0.6 124.1 %shard_map.59 = f32[2,256,128]{2,1,0:T(8,128)} custom-call(s32[2,5]{1,0:T(2,128)} %cols_hbm.1, s32[2]{0:T(128)} %count_hbm.1, bf16[2,5,128,128]{3,2,1,0:T(8,128)(2,1)} %blocks_hbm.1, bf16[256,2048]{1,0:T(8,128)(2,1)} %v_ref.1), custom_call_target="tpu_custom_call" | custom-call | tf_op jit(solution)/shard_map/pallas_call | solution.py:560
  124.7 1.7 %multiply_bitcast_fusion = (f32[256,128]{1,0:T(8,128)}, f32[256,128]{1,0:T(8,128)}) fusion(f32[2,256,128]{2,1,0:T(8,128)} %shard_map.59), kind=kLoop, calls=%fused_computation | loop fusion | flops 65536 | bytes 524288 | tf_op jit(solution)/shard_map/mul | solution.py:601

commit v7 on v6

--- a/solution.py
+++ b/solution.py
@@ -301,7 +301,7 @@
             update(step, pairs - step + i)
             return carry
 
-        lax.fori_loop(0, out, outside, 0, unroll=3)
+        lax.fori_loop(0, out, outside, 0, unroll=out)
 
     part = 4 * edge
     width = blk
@@ -343,15 +343,11 @@
     spread(1)
     f_copies[3].wait_recv()
     spread(3)
-    own_up[0].wait_recv()
-    fwd_up[0].start()
     f_copies[2].wait_recv()
     spread(2)
     for e in (1, 3, 2):
         lo_copies[e].start()
         hi_copies[e].start()
-    own_dn[1].wait_recv()
-    fwd_dn[1].start()
 
     def apply(q):
         rows = pl.ds(q * edge, edge)
@@ -359,26 +355,38 @@
         aown[rows, :] = applied.astype(jnp.bfloat16).T
         fown[rows, :] = ftx[:, pl.ds((q + 1) * edge, edge)].T
 
+    for e in (0, 1, 3):
+        own_up[e].wait_recv()
+        own_dn[e].wait_recv()
+    fwd_up[0].start()
+    fwd_dn[1].start()
     apply(1)
     apply(2)
-    own_up[3].wait_recv()
+    own_up[2].wait_recv()
+    own_dn[2].wait_recv()
     fwd_up[3].start()
+    fwd_dn[2].start()
     for e in (1, 3, 2):
         lo_copies[e].wait_recv()
         hi_copies[e].wait_recv()
     apply(0)
     apply(3)
 
-    core_copies = [remote(away.at[j], core_in.at[j], core_s.at[j], core_r.at[j], partner) for j in range(4)]
-    far = (y - z + 4) % 4 == 2
-
-    def sum_copy(j, d):
-        src, dst = share.at[j, :, :, lanes((x + d) % 4, width)], x_in.at[j, d - 1]
-        if j < 3:
-            src, dst = share.at[j, 1, :, lanes((x + d) % 4, width)], x_in.at[j, d - 1, 1]
-        return remote(src, dst, x_s.at[j, d - 1], x_r.at[j, d - 1], on_x(d))
-
-    x_copies = [[sum_copy(j, d) for d in (1, 2, 3)] for j in range(4)]
+    core_copies = [
+        [remote(away.at[j, m], core_in.at[j, m], core_s.at[j, m], core_r.at[j, m], partner) for m in range(2)]
+        for j in range(4)
+    ]
+    far = (y - z + 4) % 4 >= 2
+
+    over_z_first = [(0, 0), (1, 0)]
+    x_copies = {
+        (j, m): [
+            remote(share.at[j, m, :, lanes((x + d) % 4, width)], x_in.at[j, d - 1, m], x_s.at[j, m, d - 1],
+                   x_r.at[j, m, d - 1], on_x(d))
+            for d in (1, 2, 3)
+        ]
+        for j in range(4) for m in range(2) if (j, m) not in over_z_first
+    }
     kx_copies = [
         remote(ksum.at[:, lanes((x + d) % 4, width)], kx_in.at[d - 1], kx_s.at[d - 1], kx_r.at[d - 1], on_x(d))
         for d in (1, 2, 3)
@@ -387,80 +395,75 @@
     def to_owner(j):
         return (y + (0, 3, 1, 2)[j] - z + 4) % 4
 
-    def z_copy(j):
+    def z_copy(j, m):
         d = to_owner(j)
-        src, dst = (done.at[j], fin.at[d]) if j == 3 else (done.at[j, 1], fin.at[d, 1])
-        return d, remote(src, dst, z_s.at[j], z_r.at[d], on_z(d))
-
-    def zk_copy(j):
-        d = to_owner(j)
-        return d, remote(share.at[j, 0], zin.at[d], zk_s.at[j], zk_r.at[d], on_z(d))
+        if (j, m) in over_z_first:
+            return d, remote(share.at[j, 0], zin.at[d], zk_s.at[j], zk_r.at[d], on_z(d))
+        return d, remote(done.at[j, m], fin.at[d, m], z_s.at[j, m], z_r.at[d, m], on_z(d))
+
+    def send_over_z(j, m):
+        d, copy = z_copy(j, m)
+
+        @pl.when(d != 0)
+        def _():
+            copy.start()
+
+        @pl.when(d == 0)
+        def _():
+            if (j, m) in over_z_first:
+                zin[0] = share[j, 0]
+            else:
+                fin[0, m] = done[j, m]
 
     def half_tile(j, g):
         target_k = x // 2 if g == 0 else 1 - x // 2
         rows = lanes(target_k, half)
         lhs = ftx[rows, inner] if j == 0 else ft[j - 1, rows, :]
-        parts = [jnp.dot(lhs, rhs[...], preferred_element_type=jnp.float32) for rhs in (aown, fown)]
-
-        @pl.when(target_k == k)
-        def _():
-            for m in range(2):
-                keep[j, m] = parts[m]
-
-        @pl.when(target_k != k)
-        def _():
-            for m in range(2):
-                away[j, m] = parts[m].astype(jnp.bfloat16)
-            core_copies[j].start()
+        for m, rhs in enumerate((aown, fown)):
+            product = jnp.dot(lhs, rhs[...], preferred_element_type=jnp.float32)
+
+            @pl.when(target_k == k)
+            def _():
+                keep[j, m] = product
+
+            @pl.when(target_k != k)
+            def _():
+                away[j, m] = product.astype(jnp.bfloat16)
+                core_copies[j][m].start()
 
     def tile(j):
         half_tile(j, 0)
         half_tile(j, 1)
 
     def over_core(j):
-        core_copies[j].wait_recv()
-        share[j] = (keep[j] + core_in[j].astype(jnp.float32)).astype(jnp.bfloat16)
-        for copy in x_copies[j]:
-            copy.start()
-        if j < 3:
-            d, copy = zk_copy(j)
-
-            @pl.when(d != 0)
-            def _():
-                copy.start()
-
-            @pl.when(d == 0)
-            def _():
-                zin[0] = share[j, 0]
+        for m in range(2):
+            core_copies[j][m].wait_recv()
+            share[j, m] = (keep[j, m] + core_in[j, m].astype(jnp.float32)).astype(jnp.bfloat16)
+            if (j, m) in over_z_first:
+                send_over_z(j, m)
+            else:
+                for copy in x_copies[j, m]:
+                    copy.start()
+
+    def add_up(first, rest):
+        total = first.astype(jnp.float32)
+        for term in rest:
+            total = total + term.astype(jnp.float32)
+        return total
 
     def over_x(j):
-        for copy in x_copies[j]:
-            copy.wait_recv()
-        for m in (0, 1) if j == 3 else (1,):
-            total = share[j, m, :, lanes(x, width)].astype(jnp.float32)
-            for i in range(3):
-                total = total + x_in[j, i, m].astype(jnp.float32)
+        for m in range(2):
+            if (j, m) in over_z_first:
+                continue
+            for copy in x_copies[j, m]:
+                copy.wait_recv()
+            total = add_up(share[j, m, :, lanes(x, width)], [x_in[j, i, m] for i in range(3)])
             done[j, m] = total.astype(jnp.bfloat16)
-        d, copy = z_copy(j)
-
-        @pl.when(d != 0)
-        def _():
-            copy.start()
-
-        @pl.when(d == 0)
-        def _():
-            for m in (0, 1) if j == 3 else (1,):
-                fin[0, m] = done[j, m]
+            send_over_z(j, m)
 
     tile(0)
-    own_dn[2].wait_recv()
-    fwd_dn[2].start()
-    own_up[1].wait_recv()
-    own_up[2].wait_recv()
     tile(1)
     over_core(0)
-    own_dn[0].wait_recv()
-    own_dn[3].wait_recv()
     tile(2)
     over_core(1)
     over_x(0)
@@ -488,36 +491,28 @@
     def _():
         for d in (1, 2, 3):
             remote(share.at[0, 0], zin.at[d], zk_s.at[0], zk_r.at[d], on_z(d)).wait_recv()
-        total = zin[0].astype(jnp.float32)
-        for d in (1, 2, 3):
-            total = total + zin[d].astype(jnp.float32)
-        ksum[...] = total.astype(jnp.bfloat16)
+        ksum[...] = add_up(zin[0], [zin[d] for d in (1, 2, 3)]).astype(jnp.bfloat16)
         for copy in kx_copies:
             copy.start()
 
     over_x(3)
 
-    def add_up(first, rest):
-        total = first.astype(jnp.float32)
-        for term in rest:
-            total = total + term.astype(jnp.float32)
-        return total
+    def owned(m):
+        for d in (1, 2, 3):
+            remote(done.at[0, m], fin.at[d, m], z_s.at[0, m], z_r.at[d, m], on_z(d)).wait_recv()
+        return add_up(fin[0, m], [fin[d, m] for d in (1, 2, 3)])
 
     @pl.when(jnp.logical_not(far))
     def _():
-        for d in (1, 2, 3):
-            remote(done.at[0, 1], fin.at[d, 1], z_s.at[0], z_r.at[d], on_z(d)).wait_recv()
         for copy in kx_copies:
             copy.wait_recv()
         sums[0] = add_up(ksum[:, lanes(x, width)], [kx_in[i] for i in range(3)])
 
     @pl.when(far)
     def _():
-        for d in (1, 2, 3):
-            remote(done.at[3], fin.at[d], z_s.at[3], z_r.at[d], on_z(d)).wait_recv()
-        sums[0] = add_up(fin[0, 0], [fin[d, 0] for d in (1, 2, 3)])
-
-    sums[1] = add_up(fin[0, 1], [fin[d, 1] for d in (1, 2, 3)])
+        sums[0] = owned(0)
+
+    sums[1] = owned(1)
 
     for h in range(2):
         for copy in (*stage1[h], *(c for copies in stage2[h] for c in copies)):
@@ -530,10 +525,13 @@
         vector_up(p + pairs - out).wait_send()
         vector_down(p).wait_send()
     for copy in (*v_copies, *f_copies.values(), *lo_copies.values(), *hi_copies.values(), *own_up,
-                 *own_dn, *fwd_up.values(), *fwd_dn.values(), *core_copies, *(c for cs in x_copies for c in cs)):
+                 *own_dn, *fwd_up.values(), *fwd_dn.values(), *(c for cs in core_copies for c in cs),
+                 *(c for cs in x_copies.values() for c in cs)):
         copy.wait_send()
     for j in range(4):
-        for d, copy in [z_copy(j)] + ([zk_copy(j)] if j < 3 else []):
+        for m in range(2):
+            d, copy = z_copy(j, m)
+
             @pl.when(d != 0)
             def _():
                 copy.wait_send()
@@ -591,8 +589,8 @@
             dma((REACH_IN, 2)), dma((REACH_IN, 2)), dma((REACH_IN - 1, 2)), dma((REACH_IN - 1, 2)),
             dma((3,)), dma((3,)), dma((3,)), dma((3,)), dma((3,)), dma((3,)),
             dma((6,)), dma((6,)), dma((6,)), dma((6,)),
-            dma((4,)), dma((4,)), dma((4, 3)), dma((4, 3)), dma((4,)), dma((4,)),
-            dma((3,)), dma((4,)), dma((3,)), dma((3,)),
+            dma((4, 2)), dma((4, 2)), dma((4, 2, 3)), dma((4, 2, 3)), dma((4, 2)), dma((4, 2)),
+            dma((2,)), dma((4,)), dma((3,)), dma((3,)),
         ],
         compiler_params=pltpu.CompilerParams(
             collective_id=0, has_side_effects=True, vmem_limit_bytes=58 * 1024 * 1024

time: 129 us -> 125 us (0.969); the launches traced: 126 us -> 125 us
  Pallas kernels: 124 us -> 122 us
    pallas_call x1, Pallas kernels: 124 us -> 122 us  [body(): pl.pallas_call(functools.partial(kernel, n_row, local_blocks * n_row * n_...]
where the time goes in v7:
time: 125 us
  Pallas kernels  122 us (98%)
  other arithmetic  1.69 us (1%)
    pallas_call x1, Pallas kernels, body(): pl.pallas_call(functools.partial(kernel, n_row, local_blocks * n_row * n_...  122 us

profile of v7, /device:TPU:16, one launch (start us, length us, event | category | flops | bytes accessed | tf_op | source)
XLA Modules:
  0.0 124.8 jit_solution(15173304250298568677)
XLA Ops:
  0.6 122.4 %shard_map.59 = f32[2,256,128]{2,1,0:T(8,128)} custom-call(s32[2,5]{1,0:T(2,128)} %cols_hbm.1, s32[2]{0:T(128)} %count_hbm.1, bf16[2,5,128,128]{3,2,1,0:T(8,128)(2,1)} %blocks_hbm.1, bf16[256,2048]{1,0:T(8,128)(2,1)} %v_ref.1), custom_call_target="tpu_custom_call" | custom-call | tf_op jit(solution)/shard_map/pallas_call | solution.py:558
  123.1 1.7 %multiply_bitcast_fusion = (f32[256,128]{1,0:T(8,128)}, f32[256,128]{1,0:T(8,128)}) fusion(f32[2,256,128]{2,1,0:T(8,128)} %shard_map.59), kind=kLoop, calls=%fused_computation | loop fusion | flops 65536 | bytes 524288 | tf_op jit(solution)/shard_map/mul | solution.py:599

commit v8 on v7

--- a/solution.py
+++ b/solution.py
@@ -328,8 +328,18 @@
 
     own_up = [y_copy(0, 1, e, e, True) for e in range(4)]
     own_dn = [y_copy(0, 2, e, e, False) for e in range(4)]
-    fwd_up = {0: y_copy(1, 3, 0, 4, True), 3: y_copy(1, 3, 3, 5, True)}
-    fwd_dn = {1: y_copy(2, 3, 1, 4, False), 2: y_copy(2, 3, 2, 5, False)}
+    fwd_up, fwd_dn = y_copy(1, 3, 0, 4, True), y_copy(2, 3, 1, 4, False)
+
+    def late_rows(i):
+        return lanes(2 * (1 - x // 2) + i, width)
+
+    def late_copy(i, is_up):
+        sems = (up_s, up_r) if is_up else (dn_s, dn_r)
+        depth = pl.ds(0 if is_up else part // 2, part // 2)
+        return remote(ft.at[0 if is_up else 1, late_rows(i), depth], ft.at[2, late_rows(i), depth],
+                      sems[0].at[5 + i], sems[1].at[5 + i], on_y(1 if is_up else 3))
+
+    late = [[late_copy(i, is_up) for is_up in (True, False)] for i in range(2)]
 
     def spread(e):
         own_up[e].start()
@@ -358,34 +368,43 @@
     for e in (0, 1, 3):
         own_up[e].wait_recv()
         own_dn[e].wait_recv()
-    fwd_up[0].start()
-    fwd_dn[1].start()
+    fwd_up.start()
+    fwd_dn.start()
     apply(1)
     apply(2)
     own_up[2].wait_recv()
     own_dn[2].wait_recv()
-    fwd_up[3].start()
-    fwd_dn[2].start()
+    for i in range(2):
+        for copy in late[i]:
+            copy.start()
     for e in (1, 3, 2):
         lo_copies[e].wait_recv()
         hi_copies[e].wait_recv()
     apply(0)
     apply(3)
 
-    core_copies = [
-        [remote(away.at[j, m], core_in.at[j, m], core_s.at[j, m], core_r.at[j, m], partner) for m in range(2)]
-        for j in range(4)
-    ]
-    far = (y - z + 4) % 4 >= 2
+    def parts(j):
+        return range(2 if j == 3 else 1)
+
+    def part_rows(j, i):
+        return pl.ds(i * width, width) if j == 3 else pl.ds(0, half)
+
+    core_copies = {
+        (j, m, i): remote(away.at[j, m, part_rows(j, i)], core_in.at[j, m, part_rows(j, i)], core_s.at[j, m, i],
+                          core_r.at[j, m, i], partner)
+        for j in range(4) for m in range(2) for i in parts(j)
+    }
+    owner = (y - z + 4) % 4
+    far = owner >= 2
 
     over_z_first = [(0, 0), (1, 0)]
     x_copies = {
-        (j, m): [
-            remote(share.at[j, m, :, lanes((x + d) % 4, width)], x_in.at[j, d - 1, m], x_s.at[j, m, d - 1],
-                   x_r.at[j, m, d - 1], on_x(d))
+        (j, m, i): [
+            remote(share.at[j, m, part_rows(j, i), lanes((x + d) % 4, width)], x_in.at[j, d - 1, m, part_rows(j, i)],
+                   x_s.at[j, m, i, d - 1], x_r.at[j, m, i, d - 1], on_x(d))
             for d in (1, 2, 3)
         ]
-        for j in range(4) for m in range(2) if (j, m) not in over_z_first
+        for j in range(4) for m in range(2) for i in parts(j) if (j, m) not in over_z_first
     }
     kx_copies = [
         remote(ksum.at[:, lanes((x + d) % 4, width)], kx_in.at[d - 1], kx_s.at[d - 1], kx_r.at[d - 1], on_x(d))
@@ -395,14 +414,15 @@
     def to_owner(j):
         return (y + (0, 3, 1, 2)[j] - z + 4) % 4
 
-    def z_copy(j, m):
+    def z_copy(j, m, i):
         d = to_owner(j)
         if (j, m) in over_z_first:
             return d, remote(share.at[j, 0], zin.at[d], zk_s.at[j], zk_r.at[d], on_z(d))
-        return d, remote(done.at[j, m], fin.at[d, m], z_s.at[j, m], z_r.at[d, m], on_z(d))
-
-    def send_over_z(j, m):
-        d, copy = z_copy(j, m)
+        rows = part_rows(j, i)
+        return d, remote(done.at[j, m, rows], fin.at[d, m, rows], z_s.at[j, m, i], z_r.at[d, m, i], on_z(d))
+
+    def send_over_z(j, m, i):
+        d, copy = z_copy(j, m, i)
 
         @pl.when(d != 0)
         def _():
@@ -413,7 +433,18 @@
             if (j, m) in over_z_first:
                 zin[0] = share[j, 0]
             else:
-                fin[0, m] = done[j, m]
+                fin[0, m, part_rows(j, i), :] = done[j, m, part_rows(j, i), :]
+
+    def place_product(j, m, target_k, product, rows, sent):
+        @pl.when(target_k == k)
+        def _():
+            keep[j, m, rows, :] = product
+
+        @pl.when(target_k != k)
+        def _():
+            away[j, m, rows, :] = product.astype(jnp.bfloat16)
+            for i in sent:
+                core_copies[j, m, i].start()
 
     def half_tile(j, g):
         target_k = x // 2 if g == 0 else 1 - x // 2
@@ -422,27 +453,27 @@
         for m, rhs in enumerate((aown, fown)):
             product = jnp.dot(lhs, rhs[...], preferred_element_type=jnp.float32)
 
-            @pl.when(target_k == k)
-            def _():
-                keep[j, m] = product
-
-            @pl.when(target_k != k)
-            def _():
-                away[j, m] = product.astype(jnp.bfloat16)
-                core_copies[j][m].start()
+            place_product(j, m, target_k, product, pl.ds(0, half), parts(j))
+
+    def late_quarter(i):
+        lhs = ft[2, late_rows(i), :]
+        for m, rhs in enumerate((aown, fown)):
+            product = jnp.dot(lhs, rhs[...], preferred_element_type=jnp.float32)
+            place_product(3, m, 1 - x // 2, product, part_rows(3, i), [i])
 
     def tile(j):
         half_tile(j, 0)
         half_tile(j, 1)
 
-    def over_core(j):
+    def over_core(j, i=0):
+        rows = part_rows(j, i)
         for m in range(2):
-            core_copies[j][m].wait_recv()
-            share[j, m] = (keep[j, m] + core_in[j, m].astype(jnp.float32)).astype(jnp.bfloat16)
+            core_copies[j, m, i].wait_recv()
+            share[j, m, rows, :] = (keep[j, m, rows, :] + core_in[j, m, rows, :].astype(jnp.float32)).astype(jnp.bfloat16)
             if (j, m) in over_z_first:
-                send_over_z(j, m)
+                send_over_z(j, m, i)
             else:
-                for copy in x_copies[j, m]:
+                for copy in x_copies[j, m, i]:
                     copy.start()
 
     def add_up(first, rest):
@@ -451,15 +482,16 @@
             total = total + term.astype(jnp.float32)
         return total
 
-    def over_x(j):
+    def over_x(j, i=0):
+        rows = part_rows(j, i)
         for m in range(2):
             if (j, m) in over_z_first:
                 continue
-            for copy in x_copies[j, m]:
+            for copy in x_copies[j, m, i]:
                 copy.wait_recv()
-            total = add_up(share[j, m, :, lanes(x, width)], [x_in[j, i, m] for i in range(3)])
-            done[j, m] = total.astype(jnp.bfloat16)
-            send_over_z(j, m)
+            total = add_up(share[j, m, rows, lanes(x, width)], [x_in[j, n, m, rows, :] for n in range(3)])
+            done[j, m, rows, :] = total.astype(jnp.bfloat16)
+            send_over_z(j, m, i)
 
     tile(0)
     tile(1)
@@ -468,22 +500,24 @@
     over_core(1)
     over_x(0)
     over_core(2)
-    fwd_up[0].wait_recv()
-    fwd_dn[1].wait_recv()
+    fwd_up.wait_recv()
+    fwd_dn.wait_recv()
     half_tile(3, 0)
 
     @pl.when(x // 2 == k)
     def _():
-        over_core(3)
+        over_core(3, 0)
+        over_core(3, 1)
 
     over_x(1)
-    fwd_up[3].wait_recv()
-    fwd_dn[2].wait_recv()
-    half_tile(3, 1)
-
-    @pl.when(x // 2 != k)
-    def _():
-        over_core(3)
+    for i in range(2):
+        for copy in late[i]:
+            copy.wait_recv()
+        late_quarter(i)
+
+        @pl.when(x // 2 != k)
+        def _():
+            over_core(3, i)
 
     over_x(2)
 
@@ -495,11 +529,22 @@
         for copy in kx_copies:
             copy.start()
 
-    over_x(3)
+    over_x(3, 0)
+    over_x(3, 1)
 
     def owned(m):
-        for d in (1, 2, 3):
-            remote(done.at[0, m], fin.at[d, m], z_s.at[0, m], z_r.at[d, m], on_z(d)).wait_recv()
+        @pl.when(owner == 2)
+        def _():
+            for d in (1, 2, 3):
+                for i in range(2):
+                    rows = part_rows(3, i)
+                    remote(done.at[3, m, rows], fin.at[d, m, rows], z_s.at[3, m, i], z_r.at[d, m, i], on_z(d)).wait_recv()
+
+        @pl.when(owner != 2)
+        def _():
+            for d in (1, 2, 3):
+                remote(done.at[0, m], fin.at[d, m], z_s.at[0, m, 0], z_r.at[d, m, 0], on_z(d)).wait_recv()
+
         return add_up(fin[0, m], [fin[d, m] for d in (1, 2, 3)])
 
     @pl.when(jnp.logical_not(far))
@@ -525,12 +570,12 @@
         vector_up(p + pairs - out).wait_send()
         vector_down(p).wait_send()
     for copy in (*v_copies, *f_copies.values(), *lo_copies.values(), *hi_copies.values(), *own_up,
-                 *own_dn, *fwd_up.values(), *fwd_dn.values(), *(c for cs in core_copies for c in cs),
+                 *own_dn, fwd_up, fwd_dn, *late[0], *late[1], *core_copies.values(),
                  *(c for cs in x_copies.values() for c in cs)):
         copy.wait_send()
     for j in range(4):
-        for m in range(2):
-            d, copy = z_copy(j, m)
+        for m, i in [(m, i) for m in range(2) for i in parts(j)]:
+            d, copy = z_copy(j, m, i)
 
             @pl.when(d != 0)
             def _():
@@ -588,8 +633,8 @@
             dma((2, 3)), dma((2, 3)), dma((2, 4, 3)), dma((2, 4, 3)),
             dma((REACH_IN, 2)), dma((REACH_IN, 2)), dma((REACH_IN - 1, 2)), dma((REACH_IN - 1, 2)),
             dma((3,)), dma((3,)), dma((3,)), dma((3,)), dma((3,)), dma((3,)),
-            dma((6,)), dma((6,)), dma((6,)), dma((6,)),
-            dma((4, 2)), dma((4, 2)), dma((4, 2, 3)), dma((4, 2, 3)), dma((4, 2)), dma((4, 2)),
+            dma((7,)), dma((7,)), dma((7,)), dma((7,)),
+            dma((4, 2, 2)), dma((4, 2, 2)), dma((4, 2, 2, 3)), dma((4, 2, 2, 3)), dma((4, 2, 2)), dma((4, 2, 2)),
             dma((2,)), dma((4,)), dma((3,)), dma((3,)),
         ],
         compiler_params=pltpu.CompilerParams(

time: 125 us -> 125 us (level)
  no operation moved by 1% of the time
where the time goes in v8:
time: 125 us
  Pallas kernels  123 us (98%)
  other arithmetic  1.69 us (1%)
    pallas_call x1, Pallas kernels, body(): pl.pallas_call(functools.partial(kernel, n_row, local_blocks * n_row * n_...  123 us

profile of v8, /device:TPU:16, one launch (start us, length us, event | category | flops | bytes accessed | tf_op | source)
XLA Modules:
  0.0 125.0 jit_solution(9047403751894311728)
XLA Ops:
  0.6 122.7 %shard_map.59 = f32[2,256,128]{2,1,0:T(8,128)} custom-call(s32[2,5]{1,0:T(2,128)} %cols_hbm.1, s32[2]{0:T(128)} %count_hbm.1, bf16[2,5,128,128]{3,2,1,0:T(8,128)(2,1)} %blocks_hbm.1, bf16[256,2048]{1,0:T(8,128)(2,1)} %v_ref.1), custom_call_target="tpu_custom_call" | custom-call | tf_op jit(solution)/shard_map/pallas_call | solution.py:603
  123.3 1.7 %multiply_bitcast_fusion = (f32[256,128]{1,0:T(8,128)}, f32[256,128]{1,0:T(8,128)}) fusion(f32[2,256,128]{2,1,0:T(8,128)} %shard_map.59), kind=kLoop, calls=%fused_computation | loop fusion | flops 65536 | bytes 524288 | tf_op jit(solution)/shard_map/mul | solution.py:644

commit v9 on v8

--- a/solution.py
+++ b/solution.py
@@ -9,7 +9,7 @@
 from jax.sharding import PartitionSpec as P
 
 DEGREE = 8
-REACH_IN = DEGREE + 1
+REACH_IN = DEGREE
 MESH = pl.DeviceIdType.MESH
 
 filter_center = 0.25
@@ -18,10 +18,10 @@
 
 def kernel(n_row, total_blocks, cols_hbm, count_hbm, blocks_hbm, v_ref, sums,
            cols_ref, count_ref, blocks_ref, hg, band, vland, ext0, ext1, ftx, ft, aown, fown,
-           away, keep, core_in, share, x_in, done, fin, zin, ksum, kx_in,
+           away, keep, core_in, share, x_in, done, fin, zin, ksum, kx_in, fedge,
            in_sem, v_s, v_r, vh_s, vh_r, h1_s, h1_r, h2_s, h2_r, eu_s, eu_r, ed_s, ed_r,
            fx_s, fx_r, lo_s, lo_r, hi_s, hi_r, up_s, up_r, dn_s, dn_r, core_s, core_r, x_s, x_r, z_s, z_r,
-           zk_s, zk_r, kx_s, kx_r):
+           zk_s, zk_r, kx_s, kx_r, fe_s, fe_r):
     edge = v_ref.shape[0]
     blk = edge // 2
     pairs = 16
@@ -303,6 +303,9 @@
 
         lax.fori_loop(0, out, outside, 0, unroll=out)
 
+    f_up = remote(ext0.at[:, lanes(pairs - 1 + out, edge)], fedge.at[0], fe_s.at[0], fe_r.at[0], up)
+    f_down = remote(ext0.at[:, lanes(out, edge)], fedge.at[1], fe_s.at[1], fe_r.at[1], down)
+
     part = 4 * edge
     width = blk
     half = 2 * width
@@ -315,20 +318,27 @@
         return remote(ext0.at[:, lanes(pair, edge, count)], ftx.at[lanes(x, width), pl.ds(offset, count * edge)],
                       sems[0].at[e - 1], sems[1].at[e - 1], {"col": y * 4 + mate(e)})
 
-    f_copies = {e: x_copy(e, 0, 4, edge, (fx_s, fx_r)) for e in (1, 2, 3)}
+    f_copies = {
+        (e, b): x_copy(e, 2 * b, 2, edge + 2 * b * edge, (fx_s.at[b], fx_r.at[b])) for e in (1, 2, 3) for b in range(2)
+    }
     lo_copies = {e: x_copy(e, -1, 1, 0, (lo_s, lo_r)) for e in (1, 2, 3)}
     hi_copies = {e: x_copy(e, 4, 1, 5 * edge, (hi_s, hi_r)) for e in (1, 2, 3)}
     inner = pl.ds(edge, part)
 
-    def y_copy(from_slot, to_slot, e, index, is_up):
+    def y_copy(from_slot, to_slot, e, b, count, index, is_up):
         piece = lanes(mate(e), width)
         sems = (up_s, up_r) if is_up else (dn_s, dn_r)
-        src = ftx.at[piece, inner] if from_slot == 0 else ft.at[from_slot - 1, piece]
-        return remote(src, ft.at[to_slot - 1, piece], sems[0].at[index], sems[1].at[index], on_y(1 if is_up else 3))
-
-    own_up = [y_copy(0, 1, e, e, True) for e in range(4)]
-    own_dn = [y_copy(0, 2, e, e, False) for e in range(4)]
-    fwd_up, fwd_dn = y_copy(1, 3, 0, 4, True), y_copy(2, 3, 1, 4, False)
+        depth = 2 * b * edge, 2 * count * edge
+        if from_slot == 0:
+            src = ftx.at[piece, pl.ds(edge + depth[0], depth[1])]
+        else:
+            src = ft.at[from_slot - 1, piece, pl.ds(*depth)]
+        return remote(src, ft.at[to_slot - 1, piece, pl.ds(*depth)], sems[0].at[index], sems[1].at[index],
+                      on_y(1 if is_up else 3))
+
+    own_up = {(e, b): y_copy(0, 1, e, b, 1, 2 * e + b, True) for e in range(4) for b in range(2)}
+    own_dn = {(e, b): y_copy(0, 2, e, b, 1, 2 * e + b, False) for e in range(4) for b in range(2)}
+    fwd_up, fwd_dn = y_copy(1, 3, 0, 0, 2, 8, True), y_copy(2, 3, 1, 0, 2, 8, False)
 
     def late_rows(i):
         return lanes(2 * (1 - x // 2) + i, width)
@@ -337,27 +347,34 @@
         sems = (up_s, up_r) if is_up else (dn_s, dn_r)
         depth = pl.ds(0 if is_up else part // 2, part // 2)
         return remote(ft.at[0 if is_up else 1, late_rows(i), depth], ft.at[2, late_rows(i), depth],
-                      sems[0].at[5 + i], sems[1].at[5 + i], on_y(1 if is_up else 3))
+                      sems[0].at[9 + i], sems[1].at[9 + i], on_y(1 if is_up else 3))
 
     late = [[late_copy(i, is_up) for is_up in (True, False)] for i in range(2)]
 
-    def spread(e):
-        own_up[e].start()
-        own_dn[e].start()
-
-    for e in (1, 3, 2):
-        f_copies[e].start()
-    ftx[lanes(x, width), :] = ext0[:, lanes(4 * x - 1 + out, edge, 6)]
-    spread(0)
-    f_copies[1].wait_recv()
-    spread(1)
-    f_copies[3].wait_recv()
-    spread(3)
-    f_copies[2].wait_recv()
-    spread(2)
+    def spread(e, b):
+        own_up[e, b].start()
+        own_dn[e, b].start()
+
+    order = [(1, 0), (3, 0), (1, 1), (3, 1), (2, 0), (2, 1)]
+    for key in order:
+        f_copies[key].start()
+    ftx[lanes(x, width), inner] = ext0[:, lanes(4 * x + out, edge, 4)]
+    spread(0, 0)
+    spread(0, 1)
+    f_up.start()
+    f_down.start()
+    for key in order:
+        f_copies[key].wait_recv()
+        spread(*key)
+    f_up.wait()
+    f_down.wait()
+    ext0[:, lanes(out - 1, edge)] = fedge[0]
+    ext0[:, lanes(pairs + out, edge)] = fedge[1]
     for e in (1, 3, 2):
         lo_copies[e].start()
         hi_copies[e].start()
+    ftx[lanes(x, width), pl.ds(0, edge)] = ext0[:, lanes(4 * x - 1 + out, edge)]
+    ftx[lanes(x, width), pl.ds(5 * edge, edge)] = ext0[:, lanes(4 * x + 4 + out, edge)]
 
     def apply(q):
         rows = pl.ds(q * edge, edge)
@@ -366,14 +383,16 @@
         fown[rows, :] = ftx[:, pl.ds((q + 1) * edge, edge)].T
 
     for e in (0, 1, 3):
-        own_up[e].wait_recv()
-        own_dn[e].wait_recv()
+        for b in range(2):
+            own_up[e, b].wait_recv()
+            own_dn[e, b].wait_recv()
     fwd_up.start()
     fwd_dn.start()
     apply(1)
     apply(2)
-    own_up[2].wait_recv()
-    own_dn[2].wait_recv()
+    for b in range(2):
+        own_up[2, b].wait_recv()
+        own_dn[2, b].wait_recv()
     for i in range(2):
         for copy in late[i]:
             copy.start()
@@ -569,8 +588,8 @@
     for p in range(out):
         vector_up(p + pairs - out).wait_send()
         vector_down(p).wait_send()
-    for copy in (*v_copies, *f_copies.values(), *lo_copies.values(), *hi_copies.values(), *own_up,
-                 *own_dn, fwd_up, fwd_dn, *late[0], *late[1], *core_copies.values(),
+    for copy in (*v_copies, *f_copies.values(), *lo_copies.values(), *hi_copies.values(), *own_up.values(),
+                 *own_dn.values(), fwd_up, fwd_dn, *late[0], *late[1], *core_copies.values(),
                  *(c for cs in x_copies.values() for c in cs)):
         copy.wait_send()
     for j in range(4):
@@ -628,14 +647,15 @@
             pltpu.VMEM((4, half, wide), bf16),
             pltpu.VMEM((half, wide), bf16),
             pltpu.VMEM((3, half, width), bf16),
+            pltpu.VMEM((2, width, edge), bf16),
             dma((4,)),
             dma((16,)), dma((16,)), dma((2, REACH_IN)), dma((2, REACH_IN)),
             dma((2, 3)), dma((2, 3)), dma((2, 4, 3)), dma((2, 4, 3)),
             dma((REACH_IN, 2)), dma((REACH_IN, 2)), dma((REACH_IN - 1, 2)), dma((REACH_IN - 1, 2)),
-            dma((3,)), dma((3,)), dma((3,)), dma((3,)), dma((3,)), dma((3,)),
-            dma((7,)), dma((7,)), dma((7,)), dma((7,)),
+            dma((2, 3)), dma((2, 3)), dma((3,)), dma((3,)), dma((3,)), dma((3,)),
+            dma((11,)), dma((11,)), dma((11,)), dma((11,)),
             dma((4, 2, 2)), dma((4, 2, 2)), dma((4, 2, 2, 3)), dma((4, 2, 2, 3)), dma((4, 2, 2)), dma((4, 2, 2)),
-            dma((2,)), dma((4,)), dma((3,)), dma((3,)),
+            dma((2,)), dma((4,)), dma((3,)), dma((3,)), dma((2,)), dma((2,)),
         ],
         compiler_params=pltpu.CompilerParams(
             collective_id=0, has_side_effects=True, vmem_limit_bytes=58 * 1024 * 1024

time: 125 us -> 121 us (0.968)
  Pallas kernels: 123 us -> 119 us
    pallas_call x1, Pallas kernels: 123 us -> 119 us  [body(): pl.pallas_call(functools.partial(kernel, n_row, local_blocks * n_row * n_...]
where the time goes in v9:
time: 121 us
  Pallas kernels  119 us (98%)
  other arithmetic  1.69 us (1%)
    pallas_call x1, Pallas kernels, body(): pl.pallas_call(functools.partial(kernel, n_row, local_blocks * n_row * n_...  119 us

profile of v9, /device:TPU:16, one launch (start us, length us, event | category | flops | bytes accessed | tf_op | source)
XLA Modules:
  0.0 120.9 jit_solution(3387736351727099921)
XLA Ops:
  0.6 118.5 %shard_map.59 = f32[2,256,128]{2,1,0:T(8,128)} custom-call(s32[2,5]{1,0:T(2,128)} %cols_hbm.1, s32[2]{0:T(128)} %count_hbm.1, bf16[2,5,128,128]{3,2,1,0:T(8,128)(2,1)} %blocks_hbm.1, bf16[256,2048]{1,0:T(8,128)(2,1)} %v_ref.1), custom_call_target="tpu_custom_call" | custom-call | tf_op jit(solution)/shard_map/pallas_call | solution.py:622
  119.2 1.7 %multiply_bitcast_fusion = (f32[256,128]{1,0:T(8,128)}, f32[256,128]{1,0:T(8,128)}) fusion(f32[2,256,128]{2,1,0:T(8,128)} %shard_map.59), kind=kLoop, calls=%fused_computation | loop fusion | flops 65536 | bytes 524288 | tf_op jit(solution)/shard_map/mul | solution.py:664

commit v10 on v9

--- a/solution.py
+++ b/solution.py
@@ -380,14 +380,126 @@
         rows = pl.ds(q * edge, edge)
         applied = jnp.dot(ftx[:, pl.ds(q * edge, 3 * edge)], band[4 * x + q + out], preferred_element_type=jnp.float32)
         aown[rows, :] = applied.astype(jnp.bfloat16).T
-        fown[rows, :] = ftx[:, pl.ds((q + 1) * edge, edge)].T
-
+
+    def parts(j):
+        return range(2 if j == 3 else 1)
+
+    def part_rows(j, i):
+        return pl.ds(i * width, width) if j == 3 else pl.ds(0, half)
+
+    core_copies = {
+        (j, m, i): remote(away.at[j, m, part_rows(j, i)], core_in.at[j, m, part_rows(j, i)], core_s.at[j, m, i],
+                          core_r.at[j, m, i], partner)
+        for j in range(4) for m in range(2) for i in parts(j)
+    }
+    owner = (y - z + 4) % 4
+    far = owner >= 2
+
+    over_z_first = [(0, 0), (1, 0)]
+    x_copies = {
+        (j, m, i): [
+            remote(share.at[j, m, part_rows(j, i), lanes((x + d) % 4, width)], x_in.at[j, d - 1, m, part_rows(j, i)],
+                   x_s.at[j, m, i, d - 1], x_r.at[j, m, i, d - 1], on_x(d))
+            for d in (1, 2, 3)
+        ]
+        for j in range(4) for m in range(2) for i in parts(j) if (j, m) not in over_z_first
+    }
+    kx_copies = [
+        remote(ksum.at[:, lanes((x + d) % 4, width)], kx_in.at[d - 1], kx_s.at[d - 1], kx_r.at[d - 1], on_x(d))
+        for d in (1, 2, 3)
+    ]
+
+    def to_owner(j):
+        return (y + (0, 3, 1, 2)[j] - z + 4) % 4
+
+    def z_copy(j, m, i):
+        d = to_owner(j)
+        if (j, m) in over_z_first:
+            return d, remote(share.at[j, 0], zin.at[d], zk_s.at[j], zk_r.at[d], on_z(d))
+        rows = part_rows(j, i)
+        return d, remote(done.at[j, m, rows], fin.at[d, m, rows], z_s.at[j, m, i], z_r.at[d, m, i], on_z(d))
+
+    def send_over_z(j, m, i):
+        d, copy = z_copy(j, m, i)
+
+        @pl.when(d != 0)
+        def _():
+            copy.start()
+
+        @pl.when(d == 0)
+        def _():
+            if (j, m) in over_z_first:
+                zin[0] = share[j, 0]
+            else:
+                fin[0, m, part_rows(j, i), :] = done[j, m, part_rows(j, i), :]
+
+    def place_product(j, m, target_k, product, rows, sent):
+        @pl.when(target_k == k)
+        def _():
+            keep[j, m, rows, :] = product
+
+        @pl.when(target_k != k)
+        def _():
+            away[j, m, rows, :] = product.astype(jnp.bfloat16)
+            for i in sent:
+                core_copies[j, m, i].start()
+
+    def half_tile(j, g, products=(0, 1)):
+        target_k = x // 2 if g == 0 else 1 - x // 2
+        rows = lanes(target_k, half)
+        lhs = ftx[rows, inner] if j == 0 else ft[j - 1, rows, :]
+        for m in products:
+            product = jnp.dot(lhs, (aown, fown)[m][...], preferred_element_type=jnp.float32)
+            place_product(j, m, target_k, product, pl.ds(0, half), parts(j))
+
+    def late_quarter(i):
+        lhs = ft[2, late_rows(i), :]
+        for m, rhs in enumerate((aown, fown)):
+            product = jnp.dot(lhs, rhs[...], preferred_element_type=jnp.float32)
+            place_product(3, m, 1 - x // 2, product, part_rows(3, i), [i])
+
+    def tile(j, products=(0, 1)):
+        half_tile(j, 0, products)
+        half_tile(j, 1, products)
+
+    def over_core(j, i=0, products=(0, 1)):
+        rows = part_rows(j, i)
+        for m in products:
+            core_copies[j, m, i].wait_recv()
+            share[j, m, rows, :] = (keep[j, m, rows, :] + core_in[j, m, rows, :].astype(jnp.float32)).astype(jnp.bfloat16)
+            if (j, m) in over_z_first:
+                send_over_z(j, m, i)
+            else:
+                for copy in x_copies[j, m, i]:
+                    copy.start()
+
+    def add_up(first, rest):
+        total = first.astype(jnp.float32)
+        for term in rest:
+            total = total + term.astype(jnp.float32)
+        return total
+
+    def over_x(j, i=0):
+        rows = part_rows(j, i)
+        for m in range(2):
+            if (j, m) in over_z_first:
+                continue
+            for copy in x_copies[j, m, i]:
+                copy.wait_recv()
+            total = add_up(share[j, m, rows, lanes(x, width)], [x_in[j, n, m, rows, :] for n in range(3)])
+            done[j, m, rows, :] = total.astype(jnp.bfloat16)
+            send_over_z(j, m, i)
+
+    for q in range(4):
+        fown[pl.ds(q * edge, edge), :] = ftx[:, pl.ds((q + 1) * edge, edge)].T
+    tile(0, (1,))
     for e in (0, 1, 3):
         for b in range(2):
             own_up[e, b].wait_recv()
             own_dn[e, b].wait_recv()
     fwd_up.start()
     fwd_dn.start()
+    over_core(0, 0, (1,))
     apply(1)
     apply(2)
     for b in range(2):
@@ -401,120 +513,9 @@
         hi_copies[e].wait_recv()
     apply(0)
     apply(3)
-
-    def parts(j):
-        return range(2 if j == 3 else 1)
-
-    def part_rows(j, i):
-        return pl.ds(i * width, width) if j == 3 else pl.ds(0, half)
-
-    core_copies = {
-        (j, m, i): remote(away.at[j, m, part_rows(j, i)], core_in.at[j, m, part_rows(j, i)], core_s.at[j, m, i],
-                          core_r.at[j, m, i], partner)
-        for j in range(4) for m in range(2) for i in parts(j)
-    }
-    owner = (y - z + 4) % 4
-    far = owner >= 2
-
-    over_z_first = [(0, 0), (1, 0)]
-    x_copies = {
-        (j, m, i): [
-            remote(share.at[j, m, part_rows(j, i), lanes((x + d) % 4, width)], x_in.at[j, d - 1, m, part_rows(j, i)],
-                   x_s.at[j, m, i, d - 1], x_r.at[j, m, i, d - 1], on_x(d))
-            for d in (1, 2, 3)
-        ]
-        for j in range(4) for m in range(2) for i in parts(j) if (j, m) not in over_z_first
-    }
-    kx_copies = [
-        remote(ksum.at[:, lanes((x + d) % 4, width)], kx_in.at[d - 1], kx_s.at[d - 1], kx_r.at[d - 1], on_x(d))
-        for d in (1, 2, 3)
-    ]
-
-    def to_owner(j):
-        return (y + (0, 3, 1, 2)[j] - z + 4) % 4
-
-    def z_copy(j, m, i):
-        d = to_owner(j)
-        if (j, m) in over_z_first:
-            return d, remote(share.at[j, 0], zin.at[d], zk_s.at[j], zk_r.at[d], on_z(d))
-        rows = part_rows(j, i)
-        return d, remote(done.at[j, m, rows], fin.at[d, m, rows], z_s.at[j, m, i], z_r.at[d, m, i], on_z(d))
-
-    def send_over_z(j, m, i):
-        d, copy = z_copy(j, m, i)
-
-        @pl.when(d != 0)
-        def _():
-            copy.start()
-
-        @pl.when(d == 0)
-        def _():
-            if (j, m) in over_z_first:
-                zin[0] = share[j, 0]
-            else:
-                fin[0, m, part_rows(j, i), :] = done[j, m, part_rows(j, i), :]
-
-    def place_product(j, m, target_k, product, rows, sent):
-        @pl.when(target_k == k)
-        def _():
-            keep[j, m, rows, :] = product
-
-        @pl.when(target_k != k)
-        def _():
-            away[j, m, rows, :] = product.astype(jnp.bfloat16)
-            for i in sent:
-                core_copies[j, m, i].start()
-
-    def half_tile(j, g):
-        target_k = x // 2 if g == 0 else 1 - x // 2
-        rows = lanes(target_k, half)
-        lhs = ftx[rows, inner] if j == 0 else ft[j - 1, rows, :]
-        for m, rhs in enumerate((aown, fown)):
-            product = jnp.dot(lhs, rhs[...], preferred_element_type=jnp.float32)
-
-            place_product(j, m, target_k, product, pl.ds(0, half), parts(j))
-
-    def late_quarter(i):
-        lhs = ft[2, late_rows(i), :]
-        for m, rhs in enumerate((aown, fown)):
-            product = jnp.dot(lhs, rhs[...], preferred_element_type=jnp.float32)
-            place_product(3, m, 1 - x // 2, product, part_rows(3, i), [i])
-
-    def tile(j):
-        half_tile(j, 0)
-        half_tile(j, 1)
-
-    def over_core(j, i=0):
-        rows = part_rows(j, i)
-        for m in range(2):
-            core_copies[j, m, i].wait_recv()
-            share[j, m, rows, :] = (keep[j, m, rows, :] + core_in[j, m, rows, :].astype(jnp.float32)).astype(jnp.bfloat16)
-            if (j, m) in over_z_first:
-                send_over_z(j, m, i)
-            else:
-                for copy in x_copies[j, m, i]:
-                    copy.start()
-
-    def add_up(first, rest):
-        total = first.astype(jnp.float32)
-        for term in rest:
-            total = total + term.astype(jnp.float32)
-        return total
-
-    def over_x(j, i=0):
-        rows = part_rows(j, i)
-        for m in range(2):
-            if (j, m) in over_z_first:
-                continue
-            for copy in x_copies[j, m, i]:
-                copy.wait_recv()
-            total = add_up(share[j, m, rows, lanes(x, width)], [x_in[j, n, m, rows, :] for n in range(3)])
-            done[j, m, rows, :] = total.astype(jnp.bfloat16)
-            send_over_z(j, m, i)
-
-    tile(0)
+    tile(0, (0,))
     tile(1)
-    over_core(0)
+    over_core(0, 0, (0,))
     tile(2)
     over_core(1)
     over_x(0)

time: 121 us -> 119 us (0.983)
  Pallas kernels: 119 us -> 116 us
    pallas_call x1, Pallas kernels: 119 us -> 116 us  [body(): pl.pallas_call(functools.partial(kernel, n_row, local_blocks * n_row * n_...]
where the time goes in v10:
time: 119 us
  Pallas kernels  116 us (97%)
  other arithmetic  1.69 us (1%)
    pallas_call x1, Pallas kernels, body(): pl.pallas_call(functools.partial(kernel, n_row, local_blocks * n_row * n_...  116 us

profile of v10, /device:TPU:16, one launch (start us, length us, event | category | flops | bytes accessed | tf_op | source)
XLA Modules:
  0.0 118.8 jit_solution(17302978819875470416)
XLA Ops:
  0.6 116.5 %shard_map.59 = f32[2,256,128]{2,1,0:T(8,128)} custom-call(s32[2,5]{1,0:T(2,128)} %cols_hbm.1, s32[2]{0:T(128)} %count_hbm.1, bf16[2,5,128,128]{3,2,1,0:T(8,128)(2,1)} %blocks_hbm.1, bf16[256,2048]{1,0:T(8,128)(2,1)} %v_ref.1), custom_call_target="tpu_custom_call" | custom-call | tf_op jit(solution)/shard_map/pallas_call | solution.py:623
  117.1 1.7 %multiply_bitcast_fusion = (f32[256,128]{1,0:T(8,128)}, f32[256,128]{1,0:T(8,128)}) fusion(f32[2,256,128]{2,1,0:T(8,128)} %shard_map.59), kind=kLoop, calls=%fused_computation | loop fusion | flops 65536 | bytes 524288 | tf_op jit(solution)/shard_map/mul | solution.py:665

commit v11 on v10

--- a/solution.py
+++ b/solution.py
@@ -502,17 +502,17 @@
     over_core(0, 0, (1,))
     apply(1)
     apply(2)
+    for e in (1, 3, 2):
+        lo_copies[e].wait_recv()
+        hi_copies[e].wait_recv()
+    apply(0)
+    apply(3)
     for b in range(2):
         own_up[2, b].wait_recv()
         own_dn[2, b].wait_recv()
     for i in range(2):
         for copy in late[i]:
             copy.start()
-    for e in (1, 3, 2):
-        lo_copies[e].wait_recv()
-        hi_copies[e].wait_recv()
-    apply(0)
-    apply(3)
     tile(0, (0,))
     tile(1)
     over_core(0, 0, (0,))

time: 119 us -> 118 us (level)
  no operation moved by 1% of the time
where the time goes in v11:
time: 118 us
  Pallas kernels  116 us (98%)
  other arithmetic  1.69 us (1%)
    pallas_call x1, Pallas kernels, body(): pl.pallas_call(functools.partial(kernel, n_row, local_blocks * n_row * n_...  116 us

profile of v11, /device:TPU:16, one launch (start us, length us, event | category | flops | bytes accessed | tf_op | source)
XLA Modules:
  0.0 118.2 jit_solution(15309604296473188767)
XLA Ops:
  0.6 115.9 %shard_map.59 = f32[2,256,128]{2,1,0:T(8,128)} custom-call(s32[2,5]{1,0:T(2,128)} %cols_hbm.1, s32[2]{0:T(128)} %count_hbm.1, bf16[2,5,128,128]{3,2,1,0:T(8,128)(2,1)} %blocks_hbm.1, bf16[256,2048]{1,0:T(8,128)(2,1)} %v_ref.1), custom_call_target="tpu_custom_call" | custom-call | tf_op jit(solution)/shard_map/pallas_call | solution.py:623
  116.5 1.7 %multiply_bitcast_fusion = (f32[256,128]{1,0:T(8,128)}, f32[256,128]{1,0:T(8,128)}) fusion(f32[2,256,128]{2,1,0:T(8,128)} %shard_map.59), kind=kLoop, calls=%fused_computation | loop fusion | flops 65536 | bytes 524288 | tf_op jit(solution)/shard_map/mul | solution.py:665
